TPU v7x, 512 devices: a whole 4x8x8 slice. The times are simulated.
512 devices in a mesh: tok: 64 (over x, y, z_lo), voc: 8 (over z_hi, core).
Axes of the slice: x: 4, y: 8, z: 8 (z_hi: 4, z_lo: 2; z = z_hi * 2 + z_lo), core: 2. Of those that a mesh axis runs over, the one named last changes fastest.
Arguments:
- teacher_hidden: bfloat16 [65536, 4608], P(('tok', 'voc')), may hold values from -512 to 512
- student_hidden: bfloat16 [65536, 2304], P(('tok', 'voc')), may hold values from -512 to 512
- teacher_head: bfloat16 [2048, 4608], P('voc'), may hold values from -1 to 1
- student_head: bfloat16 [2304, 2048], P('tok', 'voc'), may hold values from -1 to 1
- targets: int32 [65536], P(('tok', 'voc')), may hold values from 0 to 2047
- row_mask: int32 [65536], P(('tok', 'voc')), may hold values 0 or 1
Outputs:
- row_loss: float32 [65536], P(('tok', 'voc'))
- head_grad: float32 [2304, 2048], P('tok', 'voc')
All inputs are finite; a program needn't handle non-finite values. No bound on the sum of `row_mask` on one device may be relied on, other than what follows from the above.
Results may differ from a plain program's by a relative error of at most 0.0022.
Values may be sent and summed in bfloat16 or wider, within the bound.
A program may use at most 64 MiB of HBM per device.

v0:
```python
import jax
import jax.numpy as jnp
from jax import lax
from jax.sharding import PartitionSpec as P


def per_device(teacher_hidden, student_hidden, teacher_head, student_head, targets, row_mask):
    student_full = lax.all_gather(student_head, "tok", axis=0, tiled=True)
    rows_t, rows_s = (
        lax.all_gather(teacher_hidden, "voc", axis=0, tiled=True),
        lax.all_gather(student_hidden, "voc", axis=0, tiled=True),
    )
    logits_s = jnp.einsum("rd,dv->rv", rows_s, student_full, preferred_element_type=jnp.float32)
    logits_t = jnp.einsum("rd,vd->rv", rows_t, teacher_head, preferred_element_type=jnp.float32)
    labels = lax.all_gather(jnp.stack([targets, row_mask]), "voc", axis=1, tiled=True)
    slab = teacher_head.shape[0]
    own_rows = teacher_hidden.shape[0]
    offset = lax.axis_index("voc") * slab
    column = jnp.arange(slab, dtype=jnp.int32)
    onehot = ((labels[0] - offset)[:, None] == column[None, :]).astype(jnp.float32)
    local_target = jnp.sum(onehot * logits_s, axis=1)
    top_t, top_s = lax.pmax((jnp.max(logits_t, axis=1), jnp.max(logits_s, axis=1)), "voc")
    exp_t = jnp.exp(logits_t - top_t[:, None])
    exp_s = jnp.exp(logits_s - top_s[:, None])
    sum_t, cross_sum, sum_s, target_logit = lax.psum(
        (
            jnp.sum(exp_t, axis=1),
            jnp.sum(exp_t * (logits_t - logits_s), axis=1),
            jnp.sum(exp_s, axis=1),
            local_target,
        ),
        "voc",
    )
    lse_t = top_t + jnp.log(sum_t)
    lse_s = top_s + jnp.log(sum_s)
    weight = labels[1].astype(jnp.float32)
    losses = weight * (cross_sum / sum_t - lse_t + lse_s + 0.5 * (lse_s - target_logit))
    own_loss = lax.dynamic_slice_in_dim(losses, lax.axis_index("voc") * own_rows, own_rows, 0)
    prob_t = exp_t / sum_t[:, None]
    prob_s = exp_s / sum_s[:, None]
    logit_grad = (weight[:, None] * (prob_s - prob_t + 0.5 * (prob_s - onehot))).astype(
        jnp.bfloat16
    )
    gradient = lax.psum_scatter(
        jnp.einsum("rk,rv->kv", rows_s, logit_grad, preferred_element_type=jnp.float32),
        "tok",
        scatter_dimension=0,
        tiled=True,
    )
    return (own_loss, gradient)


def solution(mesh):
    in_specs = (
        P(("tok", "voc"), None),
        P(("tok", "voc"), None),
        P("voc", None),
        P("tok", "voc"),
        P(("tok", "voc")),
        P(("tok", "voc")),
    )
    out_specs = (P(("tok", "voc")), P("tok", "voc"))
    return jax.shard_map(
        per_device, mesh=mesh, in_specs=in_specs, out_specs=out_specs, check_vma=False
    )
```

profile of v0, /device:TPU:6, one launch (start us, length us, event | category | flops | bytes accessed | tf_op | source)
XLA Modules:
  0.0 1132.8 jit_solution(5633445890522506293)
XLA Ops:
  7.2 0.0 all-gather.9.cloned.1.call-start
  7.2 0.7 all-gather.9.cloned.1.call-update
  7.9 0.0 all-gather.7.cloned.1.call-start
  8.0 0.7 all-gather.7.cloned.1.call-update
  8.7 0.0 all-gather.5.cloned.1.call-start
  8.7 0.7 all-gather.5.cloned.1.call-update
  9.4 0.0 all-reduce.5.cloned.1.call-start
  9.4 0.7 pad_add_fusion
  10.1 17.7 %all_gather.12 = s32[2,1024]{1,0:T(2,128)S(1)} all-gather(s32[2,128]{1,0:T(2,128)S(1)} %pad_add_fusion), channel_id=1, replica_groups=mesh['tok'=64,'voc'=8] {'voc'}, dimensions={1}, use_global_device_ids=true | all-gather | bytes 9216 | tf_op jit(solution)/shard_map/all_gather | solution.py:15
  27.8 265.5 %all-gather.9.cloned.1.call-done = bf16[64,36,256]{2,1,0:T(8,128)(2,1)} async-done(((bf16[1,36,256]{2,1,0:T(8,128)(2,1)}), bf16[64,36,256]{2,1,0:T(8,128)(2,1)}) %all-gather.9.cloned.1.call-update) | async-done | bytes 1179664 | tf_op jit(solution)/shard_map/all_gather | solution.py:8
  293.3 2.1 reshape.22
  295.5 79.8 %all-gather.7.cloned.1.call-done = bf16[1024,2304]{1,0:T(8,128)(2,1)} async-done(((bf16[128,2304]{1,0:T(8,128)(2,1)}), bf16[1024,2304]{1,0:T(8,128)(2,1)}) %all-gather.7.cloned.1.call-update) | async-done | bytes 4718608 | tf_op jit(solution)/shard_map/all_gather | solution.py:11
  375.3 5.4 fusion.11
  380.6 94.0 %all-gather.5.cloned.1.call-done = bf16[1024,4608]{1,0:T(8,128)(2,1)} async-done(((bf16[128,4608]{1,0:T(8,128)(2,1)}), bf16[1024,4608]{1,0:T(8,128)(2,1)}) %all-gather.5.cloned.1.call-update) | async-done | bytes 9437200 | tf_op jit(solution)/shard_map/all_gather | solution.py:10
  474.7 7.3 fusion.10
  482.0 16.5 %all-reduce.2 = (f32[1024]{0:T(1024)S(1)}, f32[1024]{0:T(1024)S(1)}) all-reduce(f32[1024]{0:T(1024)S(1)} %get-tuple-element.20, f32[1024]{0:T(1024)S(1)} %copy-done.2), channel_id=1, replica_groups=mesh['tok'=64,'voc'=8] {'voc'}, use_global_device_ids=true, to_apply=%region_1.0 | all-reduce | flops 2048 | bytes 16384 | tf_op jit(solution)/shard_map/pmax | solution.py:22
  498.5 1.8 multiply_reduce_fusion
  500.3 27.2 %all-reduce.1 = (f32[1024]{0:T(1024)S(1)}, f32[1024]{0:T(1024)S(1)}, f32[1024]{0:T(1024)S(1)}, f32[1024]{0:T(1024)S(1)}) all-reduce(f32[1024]{0:T(1024)S(1)} %get-tuple-element.10, f32[1024]{0:T(1024)S(1)} %get-tuple-element.11, f32[1024]{0:T(1024)S(1)} %get-tuple-element.9, ...), channel_id=1, replica_groups=mesh['tok'=64,'voc'=8] {'voc'}, use_global_device_ids=true, to_apply=%region_11.0 | all-reduce | flops 4096 | bytes 32768 | tf_op jit(solution)/shard_map/psum | solution.py:25
  527.5 5.9 convolution_bitcast_fusion
  533.4 1.3 dynamic-slice
  535.3 0.6 dynamic_slice.3
  535.9 588.6 %all-reduce.5.cloned.1.call-done = f32[2304,256]{0,1:T(8,128)} async-done(((f32[2304,256]{0,1:T(8,128)}), f32[2304,256]{0,1:T(8,128)}) %all-reduce.5.cloned.1.call-update) | async-done | bytes 2359312
  1124.6 1.0 constant_dynamic-slice_fusion
  1125.6 0.7 copy.10
  (9 shorter events, 0.1 us)
Async XLA Ops:
  7.2 467.5 %copy-start = (bf16[256,4608]{1,0:T(8,128)(2,1)S(1)}, bf16[256,4608]{1,0:T(8,128)(2,1)}, u32[]{:S(2)}) copy-start(bf16[256,4608]{1,0:T(8,128)(2,1)} %param.8) | copy-start | bytes 7077892
  7.2 286.1 %all-gather.9.cloned.1.call-start = ((), (), s32[]{:S(2)}) async-start(), calls=%async_computation.2 | async-start | bytes 1331200 | tf_op jit(solution)/shard_map/all_gather | solution.py:8
  7.9 367.4 %all-gather.7.cloned.1.call-start = ((), (), s32[]{:S(2)}) async-start(), calls=%async_computation.1 | async-start | bytes 5308416 | tf_op jit(solution)/shard_map/all_gather | solution.py:11
  8.7 466.0 %all-gather.5.cloned.1.call-start = ((), (), s32[]{:S(2)}) async-start(), calls=%async_computation | async-start | bytes 10616832 | tf_op jit(solution)/shard_map/all_gather | solution.py:10
  9.4 1115.2 %all-reduce.5.cloned.1.call-start = ((), (), s32[]{:S(2)}) async-start(), calls=%async_computation.3 | async-start | bytes 4718592
  380.6 101.3 %copy-start.2 = (f32[1024]{0:T(1024)S(1)}, f32[1024]{0:T(1024)}, u32[]{:S(2)}) copy-start(f32[1024]{0:T(1024)} %get-tuple-element.22) | copy-start | bytes 12292
  380.6 117.9 %copy-start.1 = (f32[1024,256]{0,1:T(8,128)S(1)}, f32[1024,256]{0,1:T(8,128)}, u32[]{:S(2)}) copy-start(f32[1024,256]{0,1:T(8,128)} %get-tuple-element.23) | copy-start | bytes 3145732
Sparse Core Ops, SparseCore 0:
  10.1 283.1 all-gather.8
  295.4 79.8 all-gather.6
  377.4 97.2 all-gather.4
  533.5 590.9 all-reduce.4
where the time goes:
time: 1150 us; the launch traced here: 1130 us
  waiting for transfers between devices  1030 us (90%)
  blocking collectives  61.4 us (5%)
  matrix products  18.5 us (2%)
  between operations  14.5 us (1%)
    unnamed x5, waiting for transfers between devices  591 us
    all_gather x1, waiting for transfers between devices, per_device(): student_full = lax.all_gather(student_head, 'tok', axis=0, tiled=True)  265 us
    all_gather x1, waiting for transfers between devices, per_device(): lax.all_gather(teacher_hidden, 'voc', axis=0, tiled=True)  94 us
    all_gather x1, waiting for transfers between devices, per_device(): lax.all_gather(student_hidden, 'voc', axis=0, tiled=True)  79.8 us
    psum x1, blocking collectives, per_device(): lax.psum((jnp.sum(exp_t, axis=1), jnp.sum(exp_t * (logits_t - logits_s),...  27.2 us
  transfers between devices with their start and end apart: 4, of which 4 were waited for; matrix products, arithmetic and copies ran while one was open for 1% of the time, Pallas kernels for 0%

commit v1 on v0

v1 whole, which is shorter than its diff:
```python
import jax
import jax.numpy as jnp
from jax import lax
from jax.experimental import pallas as pl
from jax.experimental.pallas import tpu as pltpu
from jax.sharding import PartitionSpec as P

NX, NY, NZ = 4, 8, 8
ROWS = 128
HALF = ROWS // 2
SLAB = 256
PIECE = 36
PAD = 48
WIN = 40
MESH = pl.DeviceIdType.MESH
F32 = jnp.float32
NT = (((1,), (1,)), ((), ()))


def remote(src, dst, send, recv, device):
    return pltpu.make_async_remote_copy(
        src_ref=src, dst_ref=dst, send_sem=send, recv_sem=recv, device_id=device, device_id_type=MESH
    )


def kernel(
    th, sh, tw, sw, lab_in, loss_ref, out_ref,
    rt, rs, tslab, spad, swt, et, es, lg, g, yb, zb, ow, ox, labs, stats, losses,
    loc_sem, lab_s, lab_r, tr_s, tr_r, zt_s, zt_r, zs_s, zs_r, y_s, y_r,
    x_s, x_r, f_s, f_r, b_s, b_r, st_s, st_r, ys_s, ys_r, zr_s, zr_r, o_s, o_r,
):
    tok, voc = lax.axis_index("tok"), lax.axis_index("voc")
    x, y, zl = lax.div(tok, 16), lax.rem(lax.div(tok, 2), NY), lax.rem(tok, 2)
    zh, c = lax.div(voc, 2), lax.rem(voc, 2)
    z = zh * 2 + zl
    me = x * 2 + c

    def dev(dx, dy, dz, dc):
        return ((dx * NY + dy) * 2 + lax.rem(dz, 2), lax.div(dz, 2) * 2 + dc)

    def group_dev(i):
        return dev(lax.div(i, 2), y, z, lax.rem(i, 2))

    xr, xl, xo = lax.rem(x + 1, NX), lax.rem(x + 3, NX), lax.rem(x + 2, NX)
    right, left, sib = dev(xr, y, z, c), dev(xl, y, z, c), dev(x, y, z, 1 - c)
    up, down = dev(x, lax.rem(y + 1, NY), z, c), dev(x, lax.rem(y + NY - 1, NY), z, c)
    partner = dev(zh, y, x * 2 + zl, c)
    away = x != zh

    barrier = pltpu.get_barrier_semaphore()

    def greet(k, _):
        pl.semaphore_signal(barrier, inc=1, device_id=group_dev(lax.rem(me + k, 8)), device_id_type=MESH)
        pl.semaphore_signal(barrier, inc=1, device_id=dev(x, y, lax.rem(z + k, NZ), c), device_id_type=MESH)
        return 0

    lax.fori_loop(1, 8, greet, 0)
    pl.semaphore_signal(barrier, inc=1, device_id=up, device_id_type=MESH)
    pl.semaphore_signal(barrier, inc=1, device_id=down, device_id_type=MESH)

    @pl.when(away)
    def _():
        pl.semaphore_signal(barrier, inc=1, device_id=partner, device_id_type=MESH)

    @pl.when(away)
    def _():
        pl.semaphore_wait(barrier, 17)

    @pl.when(jnp.logical_not(away))
    def _():
        pl.semaphore_wait(barrier, 16)

    t_row = pl.multiple_of(y * 32 + zl * 16, 16)

    def t_piece(ref, col):
        return ref.at[pl.ds(t_row, 16), pl.ds(pl.multiple_of(col * 1152, 128), 1152)]

    def turn(dst_col):
        src_t, dst_t = t_piece(tw, x), t_piece(tslab, dst_col)
        dst_s = spad.at[y, dst_col, zl]
        return src_t, dst_t, dst_s

    def turn_copies():
        src_t, dst_t, dst_s = turn(x)
        return (
            remote(src_t, dst_t, tr_s.at[0], tr_r.at[0], partner),
            remote(sw, dst_s, tr_s.at[1], tr_r.at[1], partner),
        )

    def turn_local():
        src_t, dst_t, dst_s = turn(x)
        return (
            pltpu.make_async_copy(src_t, dst_t, loc_sem.at[2]),
            pltpu.make_async_copy(sw, dst_s, loc_sem.at[3]),
        )

    @pl.when(away)
    def _():
        for copy in turn_copies():
            copy.start()

    @pl.when(jnp.logical_not(away))
    def _():
        for copy in turn_local():
            copy.start()

    def half(ref, block, h):
        return ref.at[block, pl.ds(h * HALF, HALF)]

    pairs = ((sh, rs), (th, rt))

    def send_own(d, h, a):
        src, dst = pairs[a]
        return remote(
            src.at[pl.ds(h * HALF, HALF)], half(dst, me, h), x_s.at[d, h, a], x_r.at[d, h, a], (right, left)[d]
        )

    def came_own(d, h, a):
        block = (xl, xr)[d] * 2 + c
        piece = half(pairs[a][1], block, h)
        return remote(piece, piece, x_s.at[d, h, a], x_r.at[d, h, a], (right, left)[d])

    def pass_on(d, a):
        block = (xl, xr)[d] * 2 + c
        piece = half(pairs[a][1], block, d)
        return remote(piece, piece, f_s.at[d, a], f_r.at[d, a], (right, left)[d])

    def came_on(d, a):
        piece = half(pairs[a][1], xo * 2 + c, d)
        return remote(piece, piece, f_s.at[d, a], f_r.at[d, a], (right, left)[d])

    def to_sib(n, block, h, a):
        piece = half(pairs[a][1], block * 2 + c, h)
        return remote(piece, piece, b_s.at[n, h, a], b_r.at[n, h, a], sib)

    def from_sib(n, block, h, a):
        piece = half(pairs[a][1], block * 2 + 1 - c, h)
        return remote(piece, piece, b_s.at[n, h, a], b_r.at[n, h, a], sib)

    def own_to_sib(h, a):
        src, dst = pairs[a]
        return remote(src.at[pl.ds(h * HALF, HALF)], half(dst, me, h), b_s.at[0, h, a], b_r.at[0, h, a], sib)

    for first in (0, 1):
        for a in (0, 1):
            send_own(0, first, a).start()
            send_own(1, 1 - first, a).start()
    own_copies = [pltpu.make_async_copy(pairs[a][0], pairs[a][1].at[me], loc_sem.at[a]) for a in (0, 1)]
    for copy in own_copies:
        copy.start()
    for h in (0, 1):
        for a in (0, 1):
            own_to_sib(h, a).start()

    def send_labels(k, _):
        to = lax.rem(me + k, 8)
        remote(lab_in, labs.at[me], lab_s.at[k], lab_r.at[me], group_dev(to)).start()
        return 0

    lax.fori_loop(1, 8, send_labels, 0)
    labs[me] = lab_in[...]

    @pl.when(away)
    def _():
        for copy in turn_copies():
            copy.wait_send()
        src_t, dst_t, dst_s = turn(zh)
        remote(dst_t, dst_t, tr_s.at[0], tr_r.at[0], partner).wait_recv()
        remote(dst_s, dst_s, tr_s.at[1], tr_r.at[1], partner).wait_recv()

    @pl.when(jnp.logical_not(away))
    def _():
        for copy in turn_local():
            copy.wait()

    def z_piece(dz):
        col, low = lax.div(dz, 2), lax.rem(dz, 2)
        rows = pl.ds(pl.multiple_of(y * 32 + low * 16, 16), 16)
        return (
            tslab.at[rows, pl.ds(pl.multiple_of(col * 1152, 128), 1152)],
            spad.at[y, col, low],
        )

    def z_copies(k, slot, index):
        to = lax.rem(z + k, NZ)
        t, s = z_piece(slot)
        d = dev(x, y, to, c)
        return remote(t, t, zt_s.at[k], zt_r.at[index], d), remote(s, s, zs_s.at[k], zs_r.at[index], d)

    def z_start(k, _):
        for copy in z_copies(k, z, z):
            copy.start()
        return 0

    def z_wait(k, _):
        other = lax.rem(z + k, NZ)
        for copy in z_copies(k, other, other):
            copy.wait_recv()
        return 0

    lax.fori_loop(1, NZ, z_start, 0)
    lax.fori_loop(1, NZ, z_wait, 0)

    def y_copies(d, step, chunk):
        to = (up, down)[d]
        sems = y_s.at[d, step, 0], y_r.at[d, step, 0], y_s.at[d, step, 1], y_r.at[d, step, 1]
        if step < 3:
            t = tslab.at[pl.ds(pl.multiple_of(chunk * 32, 32), 32)]
            s = spad.at[chunk]
        else:
            t = tslab.at[pl.ds(pl.multiple_of(chunk * 32 + 16 * d, 16), 16)]
            s = spad.at[chunk, pl.ds(2 * d, 2)]
        return remote(t, t, sems[0], sems[1], to), remote(s, s, sems[2], sems[3], to)

    def y_start(step):
        for d in (0, 1):
            chunk = lax.rem(y + (NY - step, step)[d], NY)
            for copy in y_copies(d, step, chunk):
                copy.start()

    def y_wait(step):
        for d in (0, 1):
            chunk = lax.rem(y + (NY - step - 1, step + 1)[d], NY)
            for copy in y_copies(d, step, chunk):
                copy.wait_recv()

    y_start(0)
    y_wait(0)
    y_start(1)
    for a in (0, 1):
        for d in (0, 1):
            came_own(d, d, a).wait_recv()
            pass_on(d, a).start()
            to_sib(1 + d, (xl, xr)[d], d, a).start()
    y_wait(1)
    y_start(2)
    for a in (0, 1):
        for d in (0, 1):
            came_own(d, 1 - d, a).wait_recv()
            to_sib(1 + d, (xl, xr)[d], 1 - d, a).start()
    y_wait(2)
    y_start(3)
    y_wait(3)

    r_out = lax.broadcasted_iota(jnp.int32, (4 * PAD, 4 * PIECE), 1)
    r_in = lax.broadcasted_iota(jnp.int32, (4 * PAD, 4 * PIECE), 0)
    quarter = lax.div(r_out, PIECE)
    pick = (r_in == quarter * PAD + (r_out - quarter * PIECE)).astype(jnp.bfloat16)

    for col in range(NX):
        parts = []
        for pair in range(NY // 2):
            padded = spad[2 * pair : 2 * pair + 2, col].reshape(4 * PAD, SLAB)
            parts.append(lax.dot_general(pick, padded, (((0,), (0,)), ((), ())), preferred_element_type=F32))
        swt[576 * col : 576 * (col + 1), :] = jnp.concatenate(parts, axis=0).astype(jnp.bfloat16)

    def wait_labels(k, _):
        other = lax.rem(me + k, 8)
        remote(labs.at[other], labs.at[other], lab_s.at[k], lab_r.at[other], sib).wait_recv()
        return 0

    lax.fori_loop(1, 8, wait_labels, 0)
    for copy in own_copies:
        copy.wait()
    for h in (0, 1):
        for a in (0, 1):
            from_sib(0, x, h, a).wait_recv()

    entry = lax.broadcasted_iota(jnp.int32, (SLAB, 2 * ROWS), 0) + me * SLAB

    def label_row(block, i):
        return jnp.concatenate([labs[2 * block, i : i + 1, :], labs[2 * block + 1, i : i + 1, :]], axis=1)

    def logits(block):
        rows_t = rt[pl.ds(2 * block, 2)].reshape(2 * ROWS, rt.shape[2])
        lt = lax.dot_general(tslab[...], rows_t, NT, preferred_element_type=F32)
        rows_s = rs[pl.ds(2 * block, 2)].reshape(2 * ROWS, rs.shape[2])
        ls = lax.dot_general(swt[...], rows_s, (((0,), (1,)), ((), ())), preferred_element_type=F32)
        top_t = jnp.max(lt, axis=0, keepdims=True)
        top_s = jnp.max(ls, axis=0, keepdims=True)
        exp_t, exp_s = jnp.exp(lt - top_t), jnp.exp(ls - top_s)
        hit = entry == label_row(block, 0)
        et[block] = exp_t
        es[block] = exp_s
        stats[me, block] = jnp.concatenate(
            [
                top_t,
                top_s,
                jnp.sum(exp_t, axis=0, keepdims=True),
                jnp.sum(exp_t * (lt - ls), axis=0, keepdims=True),
                jnp.sum(exp_s, axis=0, keepdims=True),
                jnp.sum(jnp.where(hit, ls, 0.0), axis=0, keepdims=True),
                jnp.zeros((2, 2 * ROWS), F32),
            ],
            axis=0,
        )

    logits(x)
    for d in (0, 1):
        for h in (0, 1):
            for a in (0, 1):
                from_sib(1 + d, (xl, xr)[d], h, a).wait_recv()
        logits((xl, xr)[d])
    for a in (0, 1):
        for d in (0, 1):
            came_on(d, a).wait_recv()
            to_sib(3, xo, d, a).start()
    for d in (0, 1):
        for a in (0, 1):
            from_sib(3, xo, d, a).wait_recv()
    logits(xo)

    def send_stats(k, _):
        remote(stats.at[me], stats.at[me], st_s.at[k], st_r.at[me], group_dev(lax.rem(me + k, 8))).start()
        return 0

    def wait_stats(k, _):
        other = lax.rem(me + k, 8)
        remote(stats.at[other], stats.at[other], st_s.at[k], st_r.at[other], sib).wait_recv()
        return 0

    lax.fori_loop(1, 8, send_stats, 0)
    lax.fori_loop(1, 8, wait_stats, 0)

    for block in range(NX):
        tops_t, tops_s = stats[:, block, 0, :], stats[:, block, 1, :]
        top_t = jnp.max(tops_t, axis=0, keepdims=True)
        top_s = jnp.max(tops_s, axis=0, keepdims=True)
        scale_t, scale_s = jnp.exp(tops_t - top_t), jnp.exp(tops_s - top_s)
        sum_t = jnp.sum(stats[:, block, 2, :] * scale_t, axis=0, keepdims=True)
        cross = jnp.sum(stats[:, block, 3, :] * scale_t, axis=0, keepdims=True)
        sum_s = jnp.sum(stats[:, block, 4, :] * scale_s, axis=0, keepdims=True)
        target = jnp.sum(stats[:, block, 5, :], axis=0, keepdims=True)
        lse_t, lse_s = top_t + jnp.log(sum_t), top_s + jnp.log(sum_s)
        weight = label_row(block, 1).astype(F32)
        loss = weight * (cross / sum_t - lse_t + lse_s + 0.5 * (lse_s - target))
        losses[2 * block] = loss[:, :ROWS]
        losses[2 * block + 1] = loss[:, ROWS:]
        prob_t = et[block] * (jnp.exp(stats[me, block, 0:1, :] - top_t) / sum_t)
        prob_s = es[block] * (jnp.exp(stats[me, block, 1:2, :] - top_s) / sum_s)
        onehot = (entry == label_row(block, 0)).astype(F32)
        grad = weight * ((prob_s - prob_t) + 0.5 * (prob_s - onehot))
        lg[:, 2 * ROWS * block : 2 * ROWS * (block + 1)] = grad.astype(jnp.bfloat16)
    loss_ref[...] = losses[me]

    def grad_tile(j, _):
        cols = pl.ds(pl.multiple_of(j * 256, 256), 256)
        rows_s = rs[:, :, cols].reshape(8 * ROWS, 256)
        g[cols, :] = lax.dot_general(rows_s.T, lg[...], NT, preferred_element_type=F32)
        return 0

    lax.fori_loop(0, g.shape[0] // 256, grad_tile, 0)

    def g_chunk(stream, chunk):
        return pl.ds(pl.multiple_of(stream * 576 + chunk * 72, 8), 72)

    def ring_copy(stream, step, src):
        return remote(
            src, yb.at[step, stream], ys_s.at[step, stream], ys_r.at[step, stream], (up, down)[stream // 2]
        )

    for stream in range(4):
        first = lax.rem(y + (NY - 1, 1)[stream // 2], NY)
        ring_copy(stream, 0, g.at[g_chunk(stream, first)]).start()

    def ring_add(stream, step):
        ring_copy(stream, step, yb.at[step, stream]).wait_recv()
        gap = step + 2
        chunk = lax.rem(y + (2 * NY - gap, gap)[stream // 2], NY)
        yb[step, stream] += g[g_chunk(stream, chunk), :]

    def ring_step(step, _):
        for stream in (0, 2, 1, 3):
            ring_add(stream, step)
            ring_copy(stream, step + 1, yb.at[step, stream]).start()
        return 0

    lax.fori_loop(0, NY - 2, ring_step, 0)
    for stream in (0, 2, 1, 3):
        ring_add(stream, NY - 2)

    def window(dz):
        return yb.at[NY - 2, lax.div(dz, 2), pl.ds(pl.multiple_of(lax.rem(dz, 2) * 32, 8), WIN)]

    def zr_start(k, _):
        to = lax.rem(z + k, NZ)
        remote(window(to), zb.at[z], zr_s.at[k], zr_r.at[z], dev(x, y, to, c)).start()
        return 0

    def zr_wait(k, _):
        other = lax.rem(z + k, NZ)
        remote(zb.at[other], zb.at[other], zr_s.at[k], zr_r.at[other], sib).wait_recv()
        return 0

    lax.fori_loop(1, NZ, zr_start, 0)
    zb[z] = window(z)[...]
    lax.fori_loop(1, NZ, zr_wait, 0)
    ow[...] = jnp.sum(zb[...], axis=0)

    @pl.when(away)
    def _():
        copy = remote(ow, ox, o_s, o_r, partner)
        copy.start()
        copy.wait()
        out_ref[...] = ox[...]

    @pl.when(jnp.logical_not(away))
    def _():
        out_ref[...] = ow[...]

    for d in (0, 1):
        for a in (0, 1):
            for h in (0, 1):
                send_own(d, h, a).wait_send()
            pass_on(d, a).wait_send()
    for a in (0, 1):
        for h in (0, 1):
            own_to_sib(h, a).wait_send()
            for n, block in ((1, xl), (2, xr), (3, xo)):
                to_sib(n, block, h, a).wait_send()
    for step in range(4):
        for d in (0, 1):
            for copy in y_copies(d, step, lax.rem(y + (NY - step, step)[d], NY)):
                copy.wait_send()

    def wait_sent(k, _):
        remote(lab_in, labs.at[me], lab_s.at[k], lab_r.at[me], sib).wait_send()
        for copy in z_copies(k, z, z):
            copy.wait_send()
        remote(stats.at[me], stats.at[me], st_s.at[k], st_r.at[me], sib).wait_send()
        remote(window(lax.rem(z + k, NZ)), zb.at[z], zr_s.at[k], zr_r.at[z], sib).wait_send()
        return 0

    lax.fori_loop(1, 8, wait_sent, 0)

    def wait_ring(step, _):
        for stream in range(4):
            ring_copy(stream, step, yb.at[step, stream]).wait_send()
        return 0

    lax.fori_loop(0, NY - 1, wait_ring, 0)


def per_device(teacher_hidden, student_hidden, teacher_head, student_head, targets, row_mask):
    dt, ds = teacher_hidden.shape[1], student_hidden.shape[1]
    bf16 = jnp.bfloat16
    labels = jnp.concatenate([targets[None], row_mask[None], jnp.zeros((6, ROWS), jnp.int32)], axis=0)
    padded = jnp.concatenate([student_head, jnp.zeros((PAD - PIECE, SLAB), bf16)], axis=0)
    dma = pltpu.SemaphoreType.DMA
    anywhere, vmem = pl.BlockSpec(memory_space=pl.ANY), pl.BlockSpec(memory_space=pltpu.VMEM)
    loss, window = pl.pallas_call(
        kernel,
        out_shape=(jax.ShapeDtypeStruct((1, ROWS), F32), jax.ShapeDtypeStruct((WIN, SLAB), F32)),
        in_specs=[anywhere, anywhere, anywhere, vmem, vmem],
        out_specs=(vmem, vmem),
        scratch_shapes=[
            pltpu.VMEM((8, ROWS, dt), bf16),
            pltpu.VMEM((8, ROWS, ds), bf16),
            pltpu.VMEM((SLAB, dt), bf16),
            pltpu.VMEM((NY, NX, 2, PAD, SLAB), bf16),
            pltpu.VMEM((ds, SLAB), bf16),
            pltpu.VMEM((NX, SLAB, 2 * ROWS), F32),
            pltpu.VMEM((NX, SLAB, 2 * ROWS), F32),
            pltpu.VMEM((SLAB, 8 * ROWS), bf16),
            pltpu.VMEM((ds, SLAB), F32),
            pltpu.VMEM((NY - 1, 4, 72, SLAB), F32),
            pltpu.VMEM((NZ, WIN, SLAB), F32),
            pltpu.VMEM((WIN, SLAB), F32),
            pltpu.VMEM((WIN, SLAB), F32),
            pltpu.VMEM((8, 8, ROWS), jnp.int32),
            pltpu.VMEM((8, NX, 8, 2 * ROWS), F32),
            pltpu.VMEM((8, 1, ROWS), F32),
            dma((4,)),
            dma((8,)), dma((8,)),
            dma((2,)), dma((2,)),
            dma((8,)), dma((8,)), dma((8,)), dma((8,)),
            dma((2, 4, 2)), dma((2, 4, 2)),
            dma((2, 2, 2)), dma((2, 2, 2)),
            dma((2, 2)), dma((2, 2)),
            dma((4, 2, 2)), dma((4, 2, 2)),
            dma((8,)), dma((8,)),
            dma((7, 4)), dma((7, 4)),
            dma((8,)), dma((8,)),
            dma, dma,
        ],
        compiler_params=pltpu.CompilerParams(
            collective_id=0, has_side_effects=True, vmem_limit_bytes=56 * 1024 * 1024
        ),
        cost_estimate=pl.CostEstimate(flops=4_900_000_000, bytes_accessed=6_000_000, transcendentals=1_000_000),
    )(teacher_hidden, student_hidden, teacher_head, padded, labels)
    low = lax.rem(lax.axis_index("tok"), 2)
    return loss.reshape(ROWS), lax.dynamic_slice_in_dim(window, low * (WIN - PIECE), PIECE, 0)


def solution(mesh):
    in_specs = (
        P(("tok", "voc"), None),
        P(("tok", "voc"), None),
        P("voc", None),
        P("tok", "voc"),
        P(("tok", "voc")),
        P(("tok", "voc")),
    )
    out_specs = (P(("tok", "voc")), P("tok", "voc"))
    return jax.shard_map(
        per_device, mesh=mesh, in_specs=in_specs, out_specs=out_specs, check_vma=False
    )
```

time: 1150 us -> 147 us (0.13)
  the two profiles are of different devices: /device:TPU:6 before, /device:TPU:4 now
where the time goes in v1:
time: 147 us; the launch traced here: 146 us
  Pallas kernels  140 us (95%)
  local copies, waits for them, and re-layouts  3.95 us (3%)
    pallas_call x1, Pallas kernels, per_device(): pl.pallas_call(kernel, out_shape=(jax.ShapeDtypeStruct((1, ROWS), F32), j...  140 us

profile of v1, /device:TPU:4, one launch (start us, length us, event | category | flops | bytes accessed | tf_op | source)
XLA Modules:
  0.0 146.4 jit_solution(3607323505233642244)
XLA Ops:
  0.6 0.1 pad.3.clone
  0.7 1.3 add_add_fusion.lab_in
  2.1 1.3 concatenate.6.sw
  3.4 140.5 %shard_map.77 = (f32[1,128]{1,0:T(1,128)}, f32[40,256]{1,0:T(8,128)}) custom-call(bf16[128,4608]{1,0:T(8,128)(2,1)} %th.1, bf16[128,2304]{1,0:T(8,128)(2,1)} %sh.1, bf16[256,4608]{1,0:T(8,128)(2,1)} %tw.1, bf16[48,256]{1,0:T(8,128)(2,1)} %concatenate.6.sw, s32[8,128]{1,0:T(8,128)} %add_add_fusion.lab_in), custom_call_target="tpu_custom_call" | custom-call | flops 4899999744 | bytes 6000000 | tf_op jit(solution)/shard_map/pallas_call | solution.py:451
  143.9 1.4 constant_dynamic-slice_fusion
  145.3 1.1 copy.9
  (1 shorter events, 0.0 us)

commit v2 on v1

--- a/solution.py
+++ b/solution.py
@@ -24,10 +24,10 @@
 
 
 def kernel(
-    th, sh, tw, sw, lab_in, loss_ref, out_ref,
-    rt, rs, tslab, spad, swt, et, es, lg, g, yb, zb, ow, ox, labs, stats, losses,
+    th, sh, tw, sw, target_in, mask_in, loss_ref, out_ref,
+    rt, rs, piece_ref, tslab, spad, swt, et, es, lg, g, yb, zb, y2, z2, ow, ox, labs, stats, losses,
     loc_sem, lab_s, lab_r, tr_s, tr_r, zt_s, zt_r, zs_s, zs_r, y_s, y_r,
-    x_s, x_r, f_s, f_r, b_s, b_r, st_s, st_r, ys_s, ys_r, zr_s, zr_r, o_s, o_r,
+    x_s, x_r, f_s, f_r, b_s, b_r, st_s, st_r, ys_s, ys_r, zq_s, zq_r, yr_s, yr_r, zr_s, zr_r, o_s, o_r,
 ):
     tok, voc = lax.axis_index("tok"), lax.axis_index("voc")
     x, y, zl = lax.div(tok, 16), lax.rem(lax.div(tok, 2), NY), lax.rem(tok, 2)
@@ -44,6 +44,7 @@
     xr, xl, xo = lax.rem(x + 1, NX), lax.rem(x + 3, NX), lax.rem(x + 2, NX)
     right, left, sib = dev(xr, y, z, c), dev(xl, y, z, c), dev(x, y, z, 1 - c)
     up, down = dev(x, lax.rem(y + 1, NY), z, c), dev(x, lax.rem(y + NY - 1, NY), z, c)
+    z_up, z_down = dev(x, y, lax.rem(z + 1, NZ), c), dev(x, y, lax.rem(z + NZ - 1, NZ), c)
     partner = dev(zh, y, x * 2 + zl, c)
     away = x != zh
 
@@ -52,23 +53,28 @@
     def greet(k, _):
         pl.semaphore_signal(barrier, inc=1, device_id=group_dev(lax.rem(me + k, 8)), device_id_type=MESH)
         pl.semaphore_signal(barrier, inc=1, device_id=dev(x, y, lax.rem(z + k, NZ), c), device_id_type=MESH)
+        pl.semaphore_signal(barrier, inc=1, device_id=dev(x, lax.rem(y + k, NY), z, c), device_id_type=MESH)
         return 0
 
     lax.fori_loop(1, 8, greet, 0)
-    pl.semaphore_signal(barrier, inc=1, device_id=up, device_id_type=MESH)
-    pl.semaphore_signal(barrier, inc=1, device_id=down, device_id_type=MESH)
 
     @pl.when(away)
     def _():
         pl.semaphore_signal(barrier, inc=1, device_id=partner, device_id_type=MESH)
 
+    own_copies = [pltpu.make_async_copy(ref, dst.at[me], loc_sem.at[a]) for a, (ref, dst) in enumerate(((sh, rs), (th, rt)))]
+    for copy in own_copies:
+        copy.start()
+    piece_ref[...] = jnp.concatenate([sw[...], jnp.zeros((PAD - PIECE, SLAB), sw.dtype)], axis=0)
+    labs[me] = jnp.concatenate([target_in[...], mask_in[...], jnp.zeros((6, ROWS), jnp.int32)], axis=0)
+
     @pl.when(away)
     def _():
-        pl.semaphore_wait(barrier, 17)
+        pl.semaphore_wait(barrier, 22)
 
     @pl.when(jnp.logical_not(away))
     def _():
-        pl.semaphore_wait(barrier, 16)
+        pl.semaphore_wait(barrier, 21)
 
     t_row = pl.multiple_of(y * 32 + zl * 16, 16)
 
@@ -84,14 +90,14 @@
         src_t, dst_t, dst_s = turn(x)
         return (
             remote(src_t, dst_t, tr_s.at[0], tr_r.at[0], partner),
-            remote(sw, dst_s, tr_s.at[1], tr_r.at[1], partner),
+            remote(piece_ref, dst_s, tr_s.at[1], tr_r.at[1], partner),
         )
 
     def turn_local():
         src_t, dst_t, dst_s = turn(x)
         return (
             pltpu.make_async_copy(src_t, dst_t, loc_sem.at[2]),
-            pltpu.make_async_copy(sw, dst_s, loc_sem.at[3]),
+            pltpu.make_async_copy(piece_ref, dst_s, loc_sem.at[3]),
         )
 
     @pl.when(away)
@@ -145,20 +151,16 @@
         for a in (0, 1):
             send_own(0, first, a).start()
             send_own(1, 1 - first, a).start()
-    own_copies = [pltpu.make_async_copy(pairs[a][0], pairs[a][1].at[me], loc_sem.at[a]) for a in (0, 1)]
-    for copy in own_copies:
-        copy.start()
     for h in (0, 1):
         for a in (0, 1):
             own_to_sib(h, a).start()
 
     def send_labels(k, _):
         to = lax.rem(me + k, 8)
-        remote(lab_in, labs.at[me], lab_s.at[k], lab_r.at[me], group_dev(to)).start()
+        remote(labs.at[me], labs.at[me], lab_s.at[k], lab_r.at[me], group_dev(to)).start()
         return 0
 
     lax.fori_loop(1, 8, send_labels, 0)
-    labs[me] = lab_in[...]
 
     @pl.when(away)
     def _():
@@ -343,70 +345,99 @@
         lg[:, 2 * ROWS * block : 2 * ROWS * (block + 1)] = grad.astype(jnp.bfloat16)
     loss_ref[...] = losses[me]
 
-    def grad_tile(j, _):
-        cols = pl.ds(pl.multiple_of(j * 256, 256), 256)
-        rows_s = rs[:, :, cols].reshape(8 * ROWS, 256)
-        g[cols, :] = lax.dot_general(rows_s.T, lg[...], NT, preferred_element_type=F32)
-        return 0
-
-    lax.fori_loop(0, g.shape[0] // 256, grad_tile, 0)
-
-    def g_chunk(stream, chunk):
-        return pl.ds(pl.multiple_of(stream * 576 + chunk * 72, 8), 72)
-
-    def ring_copy(stream, step, src):
+    half_cols = g.shape[0] // 2 * g.shape[1] * g.shape[2]
+    for j in range(2):
+        rows_s = rs[:, :, half_cols * j : half_cols * (j + 1)].reshape(8 * ROWS, half_cols)
+        tile = lax.dot_general(rows_s.T, lg[...], NT, preferred_element_type=F32)
+        g[2 * j : 2 * j + 2] = tile.reshape((2,) + g.shape[1:])
+
+    def y_ring(stream, step, src):
         return remote(
             src, yb.at[step, stream], ys_s.at[step, stream], ys_r.at[step, stream], (up, down)[stream // 2]
         )
 
-    for stream in range(4):
-        first = lax.rem(y + (NY - 1, 1)[stream // 2], NY)
-        ring_copy(stream, 0, g.at[g_chunk(stream, first)]).start()
+    def z_ring(stream, step, src):
+        return remote(
+            src, zb.at[step, stream], zq_s.at[step, stream], zq_r.at[step, stream], (z_up, z_down)[stream // 2]
+        )
+
+    def at_step(base, stream, step):
+        gap = step + 1
+        return lax.rem(base + (16 - gap, gap)[stream // 2], 8)
+
+    def y_view(stream, chunk):
+        return g.at[stream, chunk, :, pl.ds(0, 128)]
+
+    def z_view(stream, chunk):
+        low = pl.multiple_of(lax.rem(chunk, 2) * 32, 8)
+        return g.at[lax.div(chunk, 2), pl.ds(2 * stream, 2), pl.ds(low, WIN), pl.ds(128, 128)]
+
+    for stream in (0, 2, 1, 3):
+        y_ring(stream, 0, y_view(stream, at_step(y, stream, 0))).start()
+        z_ring(stream, 0, z_view(stream, at_step(z, stream, 0))).start()
 
     def ring_add(stream, step):
-        ring_copy(stream, step, yb.at[step, stream]).wait_recv()
-        gap = step + 2
-        chunk = lax.rem(y + (2 * NY - gap, gap)[stream // 2], NY)
-        yb[step, stream] += g[g_chunk(stream, chunk), :]
+        y_ring(stream, step, yb.at[step, stream]).wait_recv()
+        yb[step, stream] += y_view(stream, at_step(y, stream, step + 1))[...]
+
+    def z_add(stream, step):
+        z_ring(stream, step, zb.at[step, stream]).wait_recv()
+        zb[step, stream] += z_view(stream, at_step(z, stream, step + 1))[...]
 
     def ring_step(step, _):
         for stream in (0, 2, 1, 3):
             ring_add(stream, step)
-            ring_copy(stream, step + 1, yb.at[step, stream]).start()
+            y_ring(stream, step + 1, yb.at[step, stream]).start()
+            z_add(stream, step)
+            z_ring(stream, step + 1, zb.at[step, stream]).start()
         return 0
 
     lax.fori_loop(0, NY - 2, ring_step, 0)
     for stream in (0, 2, 1, 3):
         ring_add(stream, NY - 2)
-
-    def window(dz):
+        z_add(stream, NY - 2)
+
+    def y_done(dz):
         return yb.at[NY - 2, lax.div(dz, 2), pl.ds(pl.multiple_of(lax.rem(dz, 2) * 32, 8), WIN)]
 
-    def zr_start(k, _):
-        to = lax.rem(z + k, NZ)
-        remote(window(to), zb.at[z], zr_s.at[k], zr_r.at[z], dev(x, y, to, c)).start()
-        return 0
-
-    def zr_wait(k, _):
-        other = lax.rem(z + k, NZ)
-        remote(zb.at[other], zb.at[other], zr_s.at[k], zr_r.at[other], sib).wait_recv()
-        return 0
-
-    lax.fori_loop(1, NZ, zr_start, 0)
-    zb[z] = window(z)[...]
-    lax.fori_loop(1, NZ, zr_wait, 0)
-    ow[...] = jnp.sum(zb[...], axis=0)
+    def z_done(dy):
+        return zb.at[NZ - 2, lax.div(dy, 2), lax.rem(dy, 2)]
+
+    def last_copies(k):
+        to_z, to_y = lax.rem(z + k, NZ), lax.rem(y + k, NY)
+        return (
+            remote(y_done(to_z), y2.at[z], zr_s.at[k], zr_r.at[z], dev(x, y, to_z, c)),
+            remote(z_done(to_y), z2.at[y], yr_s.at[k], yr_r.at[y], dev(x, to_y, z, c)),
+        )
+
+    def last_start(k, _):
+        for copy in last_copies(k):
+            copy.start()
+        return 0
+
+    def last_wait(k, _):
+        from_z, from_y = lax.rem(z + k, NZ), lax.rem(y + k, NY)
+        remote(y2.at[from_z], y2.at[from_z], zr_s.at[k], zr_r.at[from_z], sib).wait_recv()
+        remote(z2.at[from_y], z2.at[from_y], yr_s.at[k], yr_r.at[from_y], sib).wait_recv()
+        return 0
+
+    lax.fori_loop(1, 8, last_start, 0)
+    y2[z] = y_done(z)[...]
+    z2[y] = z_done(y)[...]
+    lax.fori_loop(1, 8, last_wait, 0)
+    ow[...] = jnp.concatenate([jnp.sum(y2[...], axis=0), jnp.sum(z2[...], axis=0)], axis=1)
 
     @pl.when(away)
     def _():
         copy = remote(ow, ox, o_s, o_r, partner)
         copy.start()
         copy.wait()
-        out_ref[...] = ox[...]
 
     @pl.when(jnp.logical_not(away))
     def _():
-        out_ref[...] = ow[...]
+        ox[...] = ow[...]
+
+    out_ref[...] = jnp.where(zl == 0, ox[:PIECE], ox[WIN - PIECE :])
 
     for d in (0, 1):
         for a in (0, 1):
@@ -424,18 +455,20 @@
                 copy.wait_send()
 
     def wait_sent(k, _):
-        remote(lab_in, labs.at[me], lab_s.at[k], lab_r.at[me], sib).wait_send()
+        remote(labs.at[me], labs.at[me], lab_s.at[k], lab_r.at[me], sib).wait_send()
         for copy in z_copies(k, z, z):
             copy.wait_send()
         remote(stats.at[me], stats.at[me], st_s.at[k], st_r.at[me], sib).wait_send()
-        remote(window(lax.rem(z + k, NZ)), zb.at[z], zr_s.at[k], zr_r.at[z], sib).wait_send()
+        for copy in last_copies(k):
+            copy.wait_send()
         return 0
 
     lax.fori_loop(1, 8, wait_sent, 0)
 
     def wait_ring(step, _):
         for stream in range(4):
-            ring_copy(stream, step, yb.at[step, stream]).wait_send()
+            y_ring(stream, step, yb.at[step, stream]).wait_send()
+            z_ring(stream, step, zb.at[step, stream]).wait_send()
         return 0
 
     lax.fori_loop(0, NY - 1, wait_ring, 0)
@@ -444,27 +477,28 @@
 def per_device(teacher_hidden, student_hidden, teacher_head, student_head, targets, row_mask):
     dt, ds = teacher_hidden.shape[1], student_hidden.shape[1]
     bf16 = jnp.bfloat16
-    labels = jnp.concatenate([targets[None], row_mask[None], jnp.zeros((6, ROWS), jnp.int32)], axis=0)
-    padded = jnp.concatenate([student_head, jnp.zeros((PAD - PIECE, SLAB), bf16)], axis=0)
     dma = pltpu.SemaphoreType.DMA
     anywhere, vmem = pl.BlockSpec(memory_space=pl.ANY), pl.BlockSpec(memory_space=pltpu.VMEM)
-    loss, window = pl.pallas_call(
+    loss, out = pl.pallas_call(
         kernel,
-        out_shape=(jax.ShapeDtypeStruct((1, ROWS), F32), jax.ShapeDtypeStruct((WIN, SLAB), F32)),
-        in_specs=[anywhere, anywhere, anywhere, vmem, vmem],
+        out_shape=(jax.ShapeDtypeStruct((1, ROWS), F32), jax.ShapeDtypeStruct((PIECE, SLAB), F32)),
+        in_specs=[anywhere, anywhere, anywhere, vmem, vmem, vmem],
         out_specs=(vmem, vmem),
         scratch_shapes=[
             pltpu.VMEM((8, ROWS, dt), bf16),
             pltpu.VMEM((8, ROWS, ds), bf16),
+            pltpu.VMEM((PAD, SLAB), bf16),
             pltpu.VMEM((SLAB, dt), bf16),
             pltpu.VMEM((NY, NX, 2, PAD, SLAB), bf16),
             pltpu.VMEM((ds, SLAB), bf16),
             pltpu.VMEM((NX, SLAB, 2 * ROWS), F32),
             pltpu.VMEM((NX, SLAB, 2 * ROWS), F32),
             pltpu.VMEM((SLAB, 8 * ROWS), bf16),
-            pltpu.VMEM((ds, SLAB), F32),
-            pltpu.VMEM((NY - 1, 4, 72, SLAB), F32),
-            pltpu.VMEM((NZ, WIN, SLAB), F32),
+            pltpu.VMEM((NX, NY, 2 * PIECE, SLAB), F32),
+            pltpu.VMEM((NY - 1, 4, 2 * PIECE, 128), F32),
+            pltpu.VMEM((NZ - 1, 4, 2, WIN, 128), F32),
+            pltpu.VMEM((NZ, WIN, 128), F32),
+            pltpu.VMEM((NY, WIN, 128), F32),
             pltpu.VMEM((WIN, SLAB), F32),
             pltpu.VMEM((WIN, SLAB), F32),
             pltpu.VMEM((8, 8, ROWS), jnp.int32),
@@ -479,17 +513,16 @@
             dma((2, 2)), dma((2, 2)),
             dma((4, 2, 2)), dma((4, 2, 2)),
             dma((8,)), dma((8,)),
-            dma((7, 4)), dma((7, 4)),
-            dma((8,)), dma((8,)),
+            dma((7, 4)), dma((7, 4)), dma((7, 4)), dma((7, 4)),
+            dma((8,)), dma((8,)), dma((8,)), dma((8,)),
             dma, dma,
         ],
         compiler_params=pltpu.CompilerParams(
             collective_id=0, has_side_effects=True, vmem_limit_bytes=56 * 1024 * 1024
         ),
         cost_estimate=pl.CostEstimate(flops=4_900_000_000, bytes_accessed=6_000_000, transcendentals=1_000_000),
-    )(teacher_hidden, student_hidden, teacher_head, padded, labels)
-    low = lax.rem(lax.axis_index("tok"), 2)
-    return loss.reshape(ROWS), lax.dynamic_slice_in_dim(window, low * (WIN - PIECE), PIECE, 0)
+    )(teacher_hidden, student_hidden, teacher_head, student_head, targets.reshape(1, ROWS), row_mask.reshape(1, ROWS))
+    return loss.reshape(ROWS), out
 
 
 def solution(mesh):

time: 147 us -> 138 us (0.939)
  the two profiles are of different devices: /device:TPU:4 before, /device:TPU:6 now
where the time goes in v2:
time: 138 us; the launch traced here: 137 us
  Pallas kernels  134 us (97%)
  local copies, waits for them, and re-layouts  2.54 us (2%)
    pallas_call x1, Pallas kernels, per_device(): pl.pallas_call(kernel, out_shape=(jax.ShapeDtypeStruct((1, ROWS), F32), j...  134 us

profile of v2, /device:TPU:6, one launch (start us, length us, event | category | flops | bytes accessed | tf_op | source)
XLA Modules:
  0.0 136.7 jit_solution(13656128834536728122)
XLA Ops:
  0.6 133.5 %shard_map.77 = (f32[1,128]{1,0:T(1,128)}, f32[36,256]{1,0:T(8,128)}) custom-call(bf16[128,4608]{1,0:T(8,128)(2,1)} %th.1, bf16[128,2304]{1,0:T(8,128)(2,1)} %sh.1, bf16[256,4608]{1,0:T(8,128)(2,1)} %tw.1, bf16[36,256]{1,0:T(8,128)(2,1)} %sw.1, s32[1,128]{1,0:T(1,128)} %bitcast.3, s32[1,128]{1,0:T(1,128)} %bitcast.4), custom_call_target="tpu_custom_call" | custom-call | flops 4899999744 | bytes 6000000 | tf_op jit(solution)/shard_map/pallas_call | solution.py:482
  134.2 1.1 copy.10
  135.3 1.4 %copy.11 = f32[36,256]{1,0:T(8,128)} copy(f32[36,256]{1,0:T(8,128)} %get-tuple-element.9) | data formatting | bytes 73728

commit v3 on v2

--- a/solution.py
+++ b/solution.py
@@ -12,6 +12,7 @@
 PIECE = 36
 PAD = 48
 WIN = 40
+TALL, WIN16 = 80, 48
 MESH = pl.DeviceIdType.MESH
 F32 = jnp.float32
 NT = (((1,), (1,)), ((), ()))
@@ -25,9 +26,9 @@
 
 def kernel(
     th, sh, tw, sw, target_in, mask_in, loss_ref, out_ref,
-    rt, rs, piece_ref, tslab, spad, swt, et, es, lg, g, yb, zb, y2, z2, ow, ox, labs, stats, losses,
-    loc_sem, lab_s, lab_r, tr_s, tr_r, zt_s, zt_r, zs_s, zs_r, y_s, y_r,
-    x_s, x_r, f_s, f_r, b_s, b_r, st_s, st_r, ys_s, ys_r, zq_s, zq_r, yr_s, yr_r, zr_s, zr_r, o_s, o_r,
+    rt, rs, piece_ref, tslab, spad, swt, swr, rst, et, es, lg, g, gb, yq, zq, ya, za, y2, z2, ow, ox, labs, stats, late, losses,
+    loc_sem, lab_s, lab_r, tr_s, tr_r, zt_s, zt_r, zs_s, zs_r, h_s, h_r,
+    x_s, x_r, f_s, f_r, b_s, b_r, st_s, st_r, sl_s, sl_r, ys_s, ys_r, zq_s, zq_r, yr_s, yr_r, zr_s, zr_r, o_s, o_r,
 ):
     tok, voc = lax.axis_index("tok"), lax.axis_index("voc")
     x, y, zl = lax.div(tok, 16), lax.rem(lax.div(tok, 2), NY), lax.rem(tok, 2)
@@ -66,6 +67,7 @@
     for copy in own_copies:
         copy.start()
     piece_ref[...] = jnp.concatenate([sw[...], jnp.zeros((PAD - PIECE, SLAB), sw.dtype)], axis=0)
+    stats[me] = jnp.zeros(stats.shape[1:], F32)
     labs[me] = jnp.concatenate([target_in[...], mask_in[...], jnp.zeros((6, ROWS), jnp.int32)], axis=0)
 
     @pl.when(away)
@@ -83,7 +85,7 @@
 
     def turn(dst_col):
         src_t, dst_t = t_piece(tw, x), t_piece(tslab, dst_col)
-        dst_s = spad.at[y, dst_col, zl]
+        dst_s = spad.at[dst_col * 2 + zl, y]
         return src_t, dst_t, dst_s
 
     def turn_copies():
@@ -176,73 +178,65 @@
             copy.wait()
 
     def z_piece(dz):
-        col, low = lax.div(dz, 2), lax.rem(dz, 2)
-        rows = pl.ds(pl.multiple_of(y * 32 + low * 16, 16), 16)
+        rows = pl.ds(pl.multiple_of(y * 32 + lax.rem(dz, 2) * 16, 16), 16)
+        return tslab.at[rows, pl.ds(pl.multiple_of(lax.div(dz, 2) * 1152, 128), 1152)]
+
+    def z_copies(k, back):
+        dz, dy = lax.rem(z + k, NZ), lax.rem(y + k, NY)
+        sz, sy = (dz, dy) if back else (z, y)
+        t, s = z_piece(sz), spad.at[z, sy]
         return (
-            tslab.at[rows, pl.ds(pl.multiple_of(col * 1152, 128), 1152)],
-            spad.at[y, col, low],
-        )
-
-    def z_copies(k, slot, index):
-        to = lax.rem(z + k, NZ)
-        t, s = z_piece(slot)
-        d = dev(x, y, to, c)
-        return remote(t, t, zt_s.at[k], zt_r.at[index], d), remote(s, s, zs_s.at[k], zs_r.at[index], d)
+            remote(t, t, zt_s.at[k], zt_r.at[sz], dev(x, y, dz, c)),
+            remote(s, s, zs_s.at[k], zs_r.at[sy], dev(x, dy, z, c)),
+        )
 
     def z_start(k, _):
-        for copy in z_copies(k, z, z):
+        for copy in z_copies(k, False):
             copy.start()
         return 0
 
     def z_wait(k, _):
-        other = lax.rem(z + k, NZ)
-        for copy in z_copies(k, other, other):
+        for copy in z_copies(k, True):
             copy.wait_recv()
         return 0
 
     lax.fori_loop(1, NZ, z_start, 0)
     lax.fori_loop(1, NZ, z_wait, 0)
 
-    def y_copies(d, step, chunk):
-        to = (up, down)[d]
-        sems = y_s.at[d, step, 0], y_r.at[d, step, 0], y_s.at[d, step, 1], y_r.at[d, step, 1]
-        if step < 3:
-            t = tslab.at[pl.ds(pl.multiple_of(chunk * 32, 32), 32)]
-            s = spad.at[chunk]
+    def ring_copy(a, d, step, h, back):
+        gap = step + 1 if back else step
+        move = (8 - gap, gap)[d]
+        if a == 0:
+            chunk = lax.rem(y + move, NY)
+            piece = tslab.at[pl.ds(pl.multiple_of(chunk * 32 + 16 * h, 16), 16)]
         else:
-            t = tslab.at[pl.ds(pl.multiple_of(chunk * 32 + 16 * d, 16), 16)]
-            s = spad.at[chunk, pl.ds(2 * d, 2)]
-        return remote(t, t, sems[0], sems[1], to), remote(s, s, sems[2], sems[3], to)
-
-    def y_start(step):
-        for d in (0, 1):
-            chunk = lax.rem(y + (NY - step, step)[d], NY)
-            for copy in y_copies(d, step, chunk):
-                copy.start()
-
-    def y_wait(step):
-        for d in (0, 1):
-            chunk = lax.rem(y + (NY - step - 1, step + 1)[d], NY)
-            for copy in y_copies(d, step, chunk):
-                copy.wait_recv()
-
-    y_start(0)
-    y_wait(0)
-    y_start(1)
+            piece = spad.at[lax.rem(z + move, NZ), pl.ds(4 * h, 4)]
+        to = ((up, down), (z_up, z_down))[a][d]
+        return remote(piece, piece, h_s.at[a, d, step, h], h_r.at[a, d, step, h], to)
+
+    def ring_step(step):
+        for h in (0, 1):
+            for d in (0, 1):
+                for a in (0, 1):
+                    if 0 < step < 4 or (step == 4 and h == d):
+                        ring_copy(a, d, step - 1, h, True).wait_recv()
+                    if step < 3 or (step == 3 and h == d):
+                        ring_copy(a, d, step, h, False).start()
+
+    ring_step(0)
+    ring_step(1)
     for a in (0, 1):
         for d in (0, 1):
             came_own(d, d, a).wait_recv()
             pass_on(d, a).start()
             to_sib(1 + d, (xl, xr)[d], d, a).start()
-    y_wait(1)
-    y_start(2)
+    ring_step(2)
+    ring_step(3)
     for a in (0, 1):
         for d in (0, 1):
             came_own(d, 1 - d, a).wait_recv()
             to_sib(1 + d, (xl, xr)[d], 1 - d, a).start()
-    y_wait(2)
-    y_start(3)
-    y_wait(3)
+    ring_step(4)
 
     r_out = lax.broadcasted_iota(jnp.int32, (4 * PAD, 4 * PIECE), 1)
     r_in = lax.broadcasted_iota(jnp.int32, (4 * PAD, 4 * PIECE), 0)
@@ -252,9 +246,11 @@
     for col in range(NX):
         parts = []
         for pair in range(NY // 2):
-            padded = spad[2 * pair : 2 * pair + 2, col].reshape(4 * PAD, SLAB)
+            four = [spad[2 * col + low, row] for row in (2 * pair, 2 * pair + 1) for low in (0, 1)]
+            padded = jnp.concatenate(four, axis=0)
             parts.append(lax.dot_general(pick, padded, (((0,), (0,)), ((), ())), preferred_element_type=F32))
         swt[576 * col : 576 * (col + 1), :] = jnp.concatenate(parts, axis=0).astype(jnp.bfloat16)
+    swr[...] = swt[...].T
 
     def wait_labels(k, _):
         other = lax.rem(me + k, 8)
@@ -273,18 +269,19 @@
     def label_row(block, i):
         return jnp.concatenate([labs[2 * block, i : i + 1, :], labs[2 * block + 1, i : i + 1, :]], axis=1)
 
-    def logits(block):
+    def logits(block, sums):
         rows_t = rt[pl.ds(2 * block, 2)].reshape(2 * ROWS, rt.shape[2])
         lt = lax.dot_general(tslab[...], rows_t, NT, preferred_element_type=F32)
         rows_s = rs[pl.ds(2 * block, 2)].reshape(2 * ROWS, rs.shape[2])
-        ls = lax.dot_general(swt[...], rows_s, (((0,), (1,)), ((), ())), preferred_element_type=F32)
+        ls = lax.dot_general(swr[...], rows_s, NT, preferred_element_type=F32)
+        rst[:, pl.ds(pl.multiple_of(block * 2 * ROWS, 2 * ROWS), 2 * ROWS)] = rows_s.T
         top_t = jnp.max(lt, axis=0, keepdims=True)
         top_s = jnp.max(ls, axis=0, keepdims=True)
         exp_t, exp_s = jnp.exp(lt - top_t), jnp.exp(ls - top_s)
         hit = entry == label_row(block, 0)
         et[block] = exp_t
         es[block] = exp_s
-        stats[me, block] = jnp.concatenate(
+        sums[...] = jnp.concatenate(
             [
                 top_t,
                 top_s,
@@ -297,12 +294,34 @@
             axis=0,
         )
 
-    logits(x)
+    logits(x, stats.at[me, x])
     for d in (0, 1):
         for h in (0, 1):
             for a in (0, 1):
                 from_sib(1 + d, (xl, xr)[d], h, a).wait_recv()
-        logits((xl, xr)[d])
+        logits((xl, xr)[d], stats.at[me, (xl, xr)[d]])
+    def early_copy(k, slot):
+        return remote(stats.at[slot], stats.at[slot], st_s.at[k], st_r.at[slot], group_dev(lax.rem(me + k, 8)))
+
+    def late_copy(k, slot):
+        return remote(late.at[slot], late.at[slot], sl_s.at[k], sl_r.at[slot], group_dev(lax.rem(me + k, 8)))
+
+    def send_early(k, _):
+        early_copy(k, me).start()
+        return 0
+
+    def send_stats(k, _):
+        late_copy(k, me).start()
+        return 0
+
+    def wait_stats(k, _):
+        other = lax.rem(me + k, 8)
+        early_copy(k, me).wait_send()
+        early_copy(k, other).wait_recv()
+        late_copy(k, other).wait_recv()
+        return 0
+
+    lax.fori_loop(1, 8, send_early, 0)
     for a in (0, 1):
         for d in (0, 1):
             came_on(d, a).wait_recv()
@@ -310,19 +329,12 @@
     for d in (0, 1):
         for a in (0, 1):
             from_sib(3, xo, d, a).wait_recv()
-    logits(xo)
-
-    def send_stats(k, _):
-        remote(stats.at[me], stats.at[me], st_s.at[k], st_r.at[me], group_dev(lax.rem(me + k, 8))).start()
-        return 0
-
-    def wait_stats(k, _):
-        other = lax.rem(me + k, 8)
-        remote(stats.at[other], stats.at[other], st_s.at[k], st_r.at[other], sib).wait_recv()
-        return 0
+    logits(xo, late.at[me])
 
     lax.fori_loop(1, 8, send_stats, 0)
     lax.fori_loop(1, 8, wait_stats, 0)
+    for sender in range(8):
+        stats[sender, (sender // 2 + 2) % NX] = late[sender]
 
     for block in range(NX):
         tops_t, tops_s = stats[:, block, 0, :], stats[:, block, 1, :]
@@ -347,67 +359,55 @@
 
     half_cols = g.shape[0] // 2 * g.shape[1] * g.shape[2]
     for j in range(2):
-        rows_s = rs[:, :, half_cols * j : half_cols * (j + 1)].reshape(8 * ROWS, half_cols)
-        tile = lax.dot_general(rows_s.T, lg[...], NT, preferred_element_type=F32)
-        g[2 * j : 2 * j + 2] = tile.reshape((2,) + g.shape[1:])
-
-    def y_ring(stream, step, src):
-        return remote(
-            src, yb.at[step, stream], ys_s.at[step, stream], ys_r.at[step, stream], (up, down)[stream // 2]
-        )
-
-    def z_ring(stream, step, src):
-        return remote(
-            src, zb.at[step, stream], zq_s.at[step, stream], zq_r.at[step, stream], (z_up, z_down)[stream // 2]
-        )
-
-    def at_step(base, stream, step):
-        gap = step + 1
-        return lax.rem(base + (16 - gap, gap)[stream // 2], 8)
-
-    def y_view(stream, chunk):
-        return g.at[stream, chunk, :, pl.ds(0, 128)]
-
-    def z_view(stream, chunk):
-        low = pl.multiple_of(lax.rem(chunk, 2) * 32, 8)
-        return g.at[lax.div(chunk, 2), pl.ds(2 * stream, 2), pl.ds(low, WIN), pl.ds(128, 128)]
-
-    for stream in (0, 2, 1, 3):
-        y_ring(stream, 0, y_view(stream, at_step(y, stream, 0))).start()
-        z_ring(stream, 0, z_view(stream, at_step(z, stream, 0))).start()
-
-    def ring_add(stream, step):
-        y_ring(stream, step, yb.at[step, stream]).wait_recv()
-        yb[step, stream] += y_view(stream, at_step(y, stream, step + 1))[...]
-
-    def z_add(stream, step):
-        z_ring(stream, step, zb.at[step, stream]).wait_recv()
-        zb[step, stream] += z_view(stream, at_step(z, stream, step + 1))[...]
-
-    def ring_step(step, _):
-        for stream in (0, 2, 1, 3):
-            ring_add(stream, step)
-            y_ring(stream, step + 1, yb.at[step, stream]).start()
-            z_add(stream, step)
-            z_ring(stream, step + 1, zb.at[step, stream]).start()
-        return 0
-
-    lax.fori_loop(0, NY - 2, ring_step, 0)
-    for stream in (0, 2, 1, 3):
-        ring_add(stream, NY - 2)
-        z_add(stream, NY - 2)
-
-    def y_done(dz):
-        return yb.at[NY - 2, lax.div(dz, 2), pl.ds(pl.multiple_of(lax.rem(dz, 2) * 32, 8), WIN)]
-
-    def z_done(dy):
-        return zb.at[NZ - 2, lax.div(dy, 2), lax.rem(dy, 2)]
+        rows_s = rst[half_cols * j : half_cols * (j + 1), :]
+        tile = lax.dot_general(rows_s, lg[...], NT, preferred_element_type=F32)
+        tile = tile.reshape((2,) + g.shape[1:])
+        g[2 * j : 2 * j + 2] = tile
+        rest = jnp.zeros((2, NY, TALL - 2 * PIECE, SLAB), F32)
+        gb[2 * j : 2 * j + 2] = jnp.concatenate([tile, rest], axis=2).astype(jnp.bfloat16)
+
+    def low16(dz):
+        return pl.multiple_of(lax.rem(dz, 2) * 32, 16)
+
+    def sum_copies(k):
+        to_y, to_z = lax.rem(y + k, NY), lax.rem(z + k, NZ)
+        return (
+            remote(
+                gb.at[:, to_y, :, pl.ds(0, 128)], yq.at[y], ys_s.at[k], ys_r.at[y], dev(x, to_y, z, c)
+            ),
+            remote(
+                gb.at[lax.div(to_z, 2), :, pl.ds(low16(to_z), WIN16), pl.ds(128, 128)],
+                zq.at[z], zq_s.at[k], zq_r.at[z], dev(x, y, to_z, c),
+            ),
+        )
+
+    def sum_start(k, _):
+        for copy in sum_copies(k):
+            copy.start()
+        return 0
+
+    lax.fori_loop(1, 8, sum_start, 0)
+    ya[...] = g[:, y, :, :128]
+    za[...] = g[zh, :, pl.ds(pl.multiple_of(zl * 32, 8), WIN), 128:]
+
+    def sum_add(k, _):
+        from_y, from_z = lax.rem(y + k, NY), lax.rem(z + k, NZ)
+        remote(yq.at[from_y], yq.at[from_y], ys_s.at[k], ys_r.at[from_y], sib).wait_recv()
+        ya[...] += yq[from_y].astype(F32)[:, : 2 * PIECE]
+        remote(zq.at[from_z], zq.at[from_z], zq_s.at[k], zq_r.at[from_z], sib).wait_recv()
+        za[...] += zq[from_z].astype(F32)[:, :WIN]
+        return 0
+
+    lax.fori_loop(1, 8, sum_add, 0)
+
+    def part_y(dz):
+        return ya.at[lax.div(dz, 2), pl.ds(pl.multiple_of(lax.rem(dz, 2) * 32, 8), WIN)]
 
     def last_copies(k):
         to_z, to_y = lax.rem(z + k, NZ), lax.rem(y + k, NY)
         return (
-            remote(y_done(to_z), y2.at[z], zr_s.at[k], zr_r.at[z], dev(x, y, to_z, c)),
-            remote(z_done(to_y), z2.at[y], yr_s.at[k], yr_r.at[y], dev(x, to_y, z, c)),
+            remote(part_y(to_z), y2.at[z], zr_s.at[k], zr_r.at[z], dev(x, y, to_z, c)),
+            remote(za.at[to_y], z2.at[y], yr_s.at[k], yr_r.at[y], dev(x, to_y, z, c)),
         )
 
     def last_start(k, _):
@@ -422,8 +422,8 @@
         return 0
 
     lax.fori_loop(1, 8, last_start, 0)
-    y2[z] = y_done(z)[...]
-    z2[y] = z_done(y)[...]
+    y2[z] = part_y(z)[...]
+    z2[y] = za[y]
     lax.fori_loop(1, 8, last_wait, 0)
     ow[...] = jnp.concatenate([jnp.sum(y2[...], axis=0), jnp.sum(z2[...], axis=0)], axis=1)
 
@@ -451,27 +451,21 @@
                 to_sib(n, block, h, a).wait_send()
     for step in range(4):
         for d in (0, 1):
-            for copy in y_copies(d, step, lax.rem(y + (NY - step, step)[d], NY)):
-                copy.wait_send()
+            for h in (0, 1):
+                if step < 3 or h == d:
+                    for a in (0, 1):
+                        ring_copy(a, d, step, h, False).wait_send()
 
     def wait_sent(k, _):
         remote(labs.at[me], labs.at[me], lab_s.at[k], lab_r.at[me], sib).wait_send()
-        for copy in z_copies(k, z, z):
+        for copy in z_copies(k, False):
             copy.wait_send()
-        remote(stats.at[me], stats.at[me], st_s.at[k], st_r.at[me], sib).wait_send()
-        for copy in last_copies(k):
+        late_copy(k, me).wait_send()
+        for copy in sum_copies(k) + last_copies(k):
             copy.wait_send()
         return 0
 
     lax.fori_loop(1, 8, wait_sent, 0)
-
-    def wait_ring(step, _):
-        for stream in range(4):
-            y_ring(stream, step, yb.at[step, stream]).wait_send()
-            z_ring(stream, step, zb.at[step, stream]).wait_send()
-        return 0
-
-    lax.fori_loop(0, NY - 1, wait_ring, 0)
 
 
 def per_device(teacher_hidden, student_hidden, teacher_head, student_head, targets, row_mask):
@@ -489,31 +483,37 @@
             pltpu.VMEM((8, ROWS, ds), bf16),
             pltpu.VMEM((PAD, SLAB), bf16),
             pltpu.VMEM((SLAB, dt), bf16),
-            pltpu.VMEM((NY, NX, 2, PAD, SLAB), bf16),
+            pltpu.VMEM((NZ, NY, PAD, SLAB), bf16),
             pltpu.VMEM((ds, SLAB), bf16),
+            pltpu.VMEM((SLAB, ds), bf16),
+            pltpu.VMEM((ds, 8 * ROWS), bf16),
             pltpu.VMEM((NX, SLAB, 2 * ROWS), F32),
             pltpu.VMEM((NX, SLAB, 2 * ROWS), F32),
             pltpu.VMEM((SLAB, 8 * ROWS), bf16),
             pltpu.VMEM((NX, NY, 2 * PIECE, SLAB), F32),
-            pltpu.VMEM((NY - 1, 4, 2 * PIECE, 128), F32),
-            pltpu.VMEM((NZ - 1, 4, 2, WIN, 128), F32),
+            pltpu.VMEM((NX, NY, TALL, SLAB), bf16),
+            pltpu.VMEM((NY, NX, TALL, 128), bf16),
+            pltpu.VMEM((NZ, NY, WIN16, 128), bf16),
+            pltpu.VMEM((NX, 2 * PIECE, 128), F32),
+            pltpu.VMEM((NY, WIN, 128), F32),
             pltpu.VMEM((NZ, WIN, 128), F32),
             pltpu.VMEM((NY, WIN, 128), F32),
             pltpu.VMEM((WIN, SLAB), F32),
             pltpu.VMEM((WIN, SLAB), F32),
             pltpu.VMEM((8, 8, ROWS), jnp.int32),
             pltpu.VMEM((8, NX, 8, 2 * ROWS), F32),
+            pltpu.VMEM((8, 8, 2 * ROWS), F32),
             pltpu.VMEM((8, 1, ROWS), F32),
             dma((4,)),
             dma((8,)), dma((8,)),
             dma((2,)), dma((2,)),
             dma((8,)), dma((8,)), dma((8,)), dma((8,)),
-            dma((2, 4, 2)), dma((2, 4, 2)),
+            dma((2, 2, 4, 2)), dma((2, 2, 4, 2)),
             dma((2, 2, 2)), dma((2, 2, 2)),
             dma((2, 2)), dma((2, 2)),
             dma((4, 2, 2)), dma((4, 2, 2)),
-            dma((8,)), dma((8,)),
-            dma((7, 4)), dma((7, 4)), dma((7, 4)), dma((7, 4)),
+            dma((8,)), dma((8,)), dma((8,)), dma((8,)),
+            dma((8,)), dma((8,)), dma((8,)), dma((8,)),
             dma((8,)), dma((8,)), dma((8,)), dma((8,)),
             dma, dma,
         ],

time: 138 us -> 125 us (0.906)
  Pallas kernels: 134 us -> 121 us
    pallas_call x1, Pallas kernels: 134 us -> 121 us  [per_device(): pl.pallas_call(kernel, out_shape=(jax.ShapeDtypeStruct((1, ROWS), F32), j...]
where the time goes in v3:
time: 125 us; the launch traced here: 124 us
  Pallas kernels  121 us (97%)
  local copies, waits for them, and re-layouts  2.54 us (2%)
    pallas_call x1, Pallas kernels, per_device(): pl.pallas_call(kernel, out_shape=(jax.ShapeDtypeStruct((1, ROWS), F32), j...  121 us
    unnamed x2, local copies, waits for them, and re-layouts  2.54 us

profile of v3, /device:TPU:6, one launch (start us, length us, event | category | flops | bytes accessed | tf_op | source)
XLA Modules:
  0.0 124.5 jit_solution(11308175620777312694)
XLA Ops:
  0.6 121.3 %shard_map.77 = (f32[1,128]{1,0:T(1,128)}, f32[36,256]{1,0:T(8,128)}) custom-call(bf16[128,4608]{1,0:T(8,128)(2,1)} %th.1, bf16[128,2304]{1,0:T(8,128)(2,1)} %sh.1, bf16[256,4608]{1,0:T(8,128)(2,1)} %tw.1, bf16[36,256]{1,0:T(8,128)(2,1)} %sw.1, s32[1,128]{1,0:T(1,128)} %bitcast.3, s32[1,128]{1,0:T(1,128)} %bitcast.4), custom_call_target="tpu_custom_call" | custom-call | flops 4899999744 | bytes 6000000 | tf_op jit(solution)/shard_map/pallas_call | solution.py:476
  121.9 1.1 copy.10
  123.1 1.4 %copy.11 = f32[36,256]{1,0:T(8,128)} copy(f32[36,256]{1,0:T(8,128)} %get-tuple-element.9) | data formatting | bytes 73728

commit v4 on v0

v4 whole, which is shorter than its diff:
```python
import jax
import jax.numpy as jnp
from jax import lax
from jax.experimental import pallas as pl
from jax.experimental.pallas import tpu as pltpu
from jax.sharding import PartitionSpec as P

NX, NY, NZ = 4, 8, 8
ROWS = 128
PART = ROWS // 4
BLOCK = 8 * PART
SLAB = 256
PIECE = 36
PAD = 48
WIN = 40
CHUNK = 8 * PIECE
MESH = pl.DeviceIdType.MESH
F32 = jnp.float32
NT = (((1,), (1,)), ((), ()))


def remote(src, dst, send, recv, device):
    return pltpu.make_async_remote_copy(
        src_ref=src, dst_ref=dst, send_sem=send, recv_sem=recv, device_id=device, device_id_type=MESH
    )


def kernel(
    th, sh, tw, sw, target_in, mask_in, loss_ref, out_ref,
    rt, rs, piece_ref, tslab, spad, swt, swr, rst, et, es, lg, gpf, gpb, gzf, gzb, yq, zq, ya, za, y2, z2, ow, ox, labs, stats,
    loc_sem, lab_s, lab_r, tr_s, tr_r, zs_s, zs_r, h_s, h_r,
    x_s, x_r, b_s, b_r, bo_s, bo_r, st_s, st_r, ys_s, ys_r, zq_s, zq_r, yr_s, yr_r, zr_s, zr_r, o_s, o_r,
):
    tok, voc = lax.axis_index("tok"), lax.axis_index("voc")
    x, y, zl = lax.div(tok, 16), lax.rem(lax.div(tok, 2), NY), lax.rem(tok, 2)
    zh, c = lax.div(voc, 2), lax.rem(voc, 2)
    z = zh * 2 + zl
    xh, xl, yh, yl = lax.div(x, 2), lax.rem(x, 2), lax.div(y, 2), lax.rem(y, 2)
    slab = xl * 2 + yl
    me = slab * 2 + c
    p = xh * 4 + yh

    def dev(dx, dy, dz, dc):
        return ((dx * NY + dy) * 2 + lax.rem(dz, 2), lax.div(dz, 2) * 2 + dc)

    def p_dev(dp):
        return dev(lax.div(dp, 4) * 2 + xl, lax.rem(dp, 4) * 2 + yl, z, c)

    def square_xy(q, to_xl, to_yl):
        tx, ty = q // 2, q % 2
        step_x = lax.rem(xl + to_xl, 2) * (1 + 2 * lax.rem(xl + tx, 2))
        step_y = lax.rem(yl + to_yl, 2) * (1 + 6 * lax.rem(yl + ty, 2))
        return lax.rem(x + step_x, NX), lax.rem(y + step_y, NY)

    def group_dev(q, i):
        dx, dy = square_xy(q, lax.div(i, 4), lax.rem(lax.div(i, 2), 2))
        return dev(dx, dy, z, lax.rem(i, 2))

    def other_chip(m):
        return lax.rem(xl + m // 2, 2), lax.rem(yl + m % 2, 2)

    sib = dev(x, y, z, 1 - c)
    z_up, z_down = dev(x, y, lax.rem(z + 1, NZ), c), dev(x, y, lax.rem(z + NZ - 1, NZ), c)
    partner = dev(xh * 2 + lax.div(zh, 2), yh * 2 + lax.rem(zh, 2), slab * 2 + zl, c)
    away = slab != zh

    barrier = pltpu.get_barrier_semaphore()

    def hail(device):
        pl.semaphore_signal(barrier, inc=1, device_id=device, device_id_type=MESH)

    @pl.when(away)
    def _():
        hail(partner)

    hail(sib)
    for dx in (0, 1, NX - 1):
        for dy in (0, 1, NY - 1):
            if dx or dy:
                for dc in (0, 1):
                    hail(dev(lax.rem(x + dx, NX), lax.rem(y + dy, NY), z, dc))

    def greet(k, _):
        hail(dev(x, y, lax.rem(z + k, NZ), c))
        hail(p_dev(lax.rem(p + k, 8)))
        return 0

    lax.fori_loop(1, 8, greet, 0)

    pairs = ((sh, rs), (th, rt))
    own_copies = [pltpu.make_async_copy(pairs[a][0], pairs[a][1].at[:, me], loc_sem.at[a]) for a in (0, 1)]
    for copy in own_copies:
        copy.start()
    piece_ref[...] = jnp.concatenate([sw[...], jnp.zeros((PAD - PIECE, SLAB), sw.dtype)], axis=0)
    own_labels = jnp.concatenate([target_in[...], mask_in[...], jnp.zeros((6, ROWS), jnp.int32)], axis=0)
    for q in range(4):
        labs[q, me] = own_labels

    @pl.when(away)
    def _():
        pl.semaphore_wait(barrier, 32)

    @pl.when(jnp.logical_not(away))
    def _():
        pl.semaphore_wait(barrier, 31)

    def head_rows(dz):
        return pl.ds(pl.multiple_of(dz * 32, 32), 32)

    def turn(dz):
        return tw.at[head_rows(dz)], tslab.at[head_rows(dz)], spad.at[dz, p]

    def turn_copies():
        src_t, dst_t, dst_s = turn(slab * 2 + zl)
        return (
            remote(src_t, dst_t, tr_s.at[0], tr_r.at[0], partner),
            remote(piece_ref, dst_s, tr_s.at[1], tr_r.at[1], partner),
        )

    def turn_local():
        src_t, dst_t, dst_s = turn(slab * 2 + zl)
        return (
            pltpu.make_async_copy(src_t, dst_t, loc_sem.at[2]),
            pltpu.make_async_copy(piece_ref, dst_s, loc_sem.at[3]),
        )

    @pl.when(away)
    def _():
        for copy in turn_copies():
            copy.start()

    @pl.when(jnp.logical_not(away))
    def _():
        for copy in turn_local():
            copy.start()

    def send_rows(q, m, a):
        dx, dy = square_xy(q, *other_chip(m))
        src, dst = pairs[a]
        return remote(src.at[q], dst.at[q, me], x_s.at[q, m - 1, a], x_r.at[q, m - 1, a], dev(dx, dy, z, c))

    def slot_of(m, core):
        ox_, oy_ = other_chip(m)
        return (ox_ * 2 + oy_) * 2 + core

    def came_rows(q, m, a):
        part = pairs[a][1].at[q, slot_of(m, c)]
        return remote(part, part, x_s.at[q, m - 1, a], x_r.at[q, m - 1, a], sib)

    def to_sib(q, m, a):
        part = pairs[a][1].at[q, slot_of(m, c)]
        return remote(part, part, b_s.at[q, m - 1, a], b_r.at[q, m - 1, a], sib)

    def from_sib(q, m, a):
        part = pairs[a][1].at[q, slot_of(m, 1 - c)]
        return remote(part, part, b_s.at[q, m - 1, a], b_r.at[q, m - 1, a], sib)

    def own_to_sib(a):
        return remote(pairs[a][0], pairs[a][1].at[:, me], bo_s.at[a], bo_r.at[a], sib)

    def own_from_sib(a):
        part = pairs[a][1].at[:, slab * 2 + 1 - c]
        return remote(part, part, bo_s.at[a], bo_r.at[a], sib)

    for q in range(4):
        for m in (1, 2, 3):
            for a in (0, 1):
                send_rows(q, m, a).start()
    for a in (0, 1):
        own_to_sib(a).start()

    def take_rows(q):
        for a in (0, 1):
            for m in (1, 2, 3):
                came_rows(q, m, a).wait_recv()
                to_sib(q, m, a).start()

    def label_copy(q, k, slot):
        part = labs.at[q, slot]
        return remote(part, part, lab_s.at[q, k], lab_r.at[q, slot], group_dev(q, lax.rem(me + k, 8)))

    def send_labels(k, _):
        for q in range(4):
            label_copy(q, k, me).start()
        return 0

    lax.fori_loop(1, 8, send_labels, 0)

    @pl.when(away)
    def _():
        for copy in turn_copies():
            copy.wait_send()
        src_t, dst_t, dst_s = turn(z)
        remote(dst_t, dst_t, tr_s.at[0], tr_r.at[0], partner).wait_recv()
        remote(dst_s, dst_s, tr_s.at[1], tr_r.at[1], partner).wait_recv()

    @pl.when(jnp.logical_not(away))
    def _():
        for copy in turn_local():
            copy.wait()

    def p_copy(k, back):
        dp = lax.rem(p + k, 8)
        sp = dp if back else p
        piece = spad.at[z, sp]
        return remote(piece, piece, zs_s.at[k], zs_r.at[sp], p_dev(dp))

    def p_start(k, _):
        p_copy(k, False).start()
        return 0

    def p_wait(k, _):
        p_copy(k, True).wait_recv()
        return 0

    def ring_copy(a, d, step, h, back):
        gap = step + 1 if back else step
        chunk = lax.rem(z + (8 - gap, gap)[d], NZ)
        if a == 0:
            piece = tslab.at[pl.ds(pl.multiple_of(chunk * 32 + 16 * h, 16), 16)]
        else:
            piece = spad.at[chunk, pl.ds(4 * h, 4)]
        return remote(piece, piece, h_s.at[a, d, step, h], h_r.at[a, d, step, h], (z_up, z_down)[d])

    def ring_step(a, step):
        for h in (0, 1):
            for d in (0, 1):
                if 0 < step < 4 or (step == 4 and h == d):
                    ring_copy(a, d, step - 1, h, True).wait_recv()
                if step < 3 or (step == 3 and h == d):
                    ring_copy(a, d, step, h, False).start()

    lax.fori_loop(1, 8, p_start, 0)
    ring_step(0, 0)
    lax.fori_loop(1, 8, p_wait, 0)
    ring_step(1, 0)
    for step in range(1, 5):
        ring_step(0, step)
        take_rows(step - 1)
        ring_step(1, step)

    r_out = lax.broadcasted_iota(jnp.int32, (4 * PAD, 4 * PIECE), 1)
    r_in = lax.broadcasted_iota(jnp.int32, (4 * PAD, 4 * PIECE), 0)
    quarter = lax.div(r_out, PIECE)
    pick = (r_in == quarter * PAD + (r_out - quarter * PIECE)).astype(jnp.bfloat16)

    for col in range(NX):
        parts = []
        for pair in range(NY // 2):
            four = [
                spad[2 * (2 * (col % 2) + odd) + low, 4 * (col // 2) + pair] for odd in (0, 1) for low in (0, 1)
            ]
            padded = jnp.concatenate(four, axis=0)
            parts.append(lax.dot_general(pick, padded, (((0,), (0,)), ((), ())), preferred_element_type=F32))
        swt[576 * col : 576 * (col + 1), :] = jnp.concatenate(parts, axis=0).astype(jnp.bfloat16)
    swr[...] = swt[...].T

    def wait_labels(k, _):
        for q in range(4):
            label_copy(q, k, lax.rem(me + k, 8)).wait_recv()
        return 0

    lax.fori_loop(1, 8, wait_labels, 0)
    for copy in own_copies:
        copy.wait()
    for a in (0, 1):
        own_from_sib(a).wait_recv()

    entry = lax.broadcasted_iota(jnp.int32, (SLAB, BLOCK), 0) + me * SLAB

    def label_row(q, i):
        return jnp.concatenate([labs[q, slot, i : i + 1, PART * q : PART * (q + 1)] for slot in range(8)], axis=1)

    def logits(q):
        rows_t = rt[q].reshape(BLOCK, rt.shape[3])
        lt = lax.dot_general(tslab[...], rows_t, NT, preferred_element_type=F32)
        rows_s = rs[q].reshape(BLOCK, rs.shape[3])
        ls = lax.dot_general(swr[...], rows_s, NT, preferred_element_type=F32)
        rst[:, BLOCK * q : BLOCK * (q + 1)] = rows_s.T
        top_t = jnp.max(lt, axis=0, keepdims=True)
        top_s = jnp.max(ls, axis=0, keepdims=True)
        exp_t, exp_s = jnp.exp(lt - top_t), jnp.exp(ls - top_s)
        hit = entry == label_row(q, 0)
        et[q] = exp_t
        es[q] = exp_s
        stats[q, me] = jnp.concatenate(
            [
                top_t,
                top_s,
                jnp.sum(exp_t, axis=0, keepdims=True),
                jnp.sum(exp_t * (lt - ls), axis=0, keepdims=True),
                jnp.sum(exp_s, axis=0, keepdims=True),
                jnp.sum(jnp.where(hit, ls, 0.0), axis=0, keepdims=True),
                jnp.zeros((2, BLOCK), F32),
            ],
            axis=0,
        )

    def stats_copy(q, k, slot):
        part = stats.at[q, slot]
        return remote(part, part, st_s.at[q, k], st_r.at[q, slot], group_dev(q, lax.rem(me + k, 8)))

    for q in range(4):
        for m in (1, 2, 3):
            for a in (0, 1):
                from_sib(q, m, a).wait_recv()
        logits(q)

        def send_stats(k, _, q=q):
            stats_copy(q, k, me).start()
            return 0

        lax.fori_loop(1, 8, send_stats, 0)

    own_losses = []
    for block in range(4):
        def wait_stats(k, _, q=block):
            stats_copy(q, k, lax.rem(me + k, 8)).wait_recv()
            return 0

        lax.fori_loop(1, 8, wait_stats, 0)
        tops_t, tops_s = stats[block, :, 0, :], stats[block, :, 1, :]
        top_t = jnp.max(tops_t, axis=0, keepdims=True)
        top_s = jnp.max(tops_s, axis=0, keepdims=True)
        scale_t, scale_s = jnp.exp(tops_t - top_t), jnp.exp(tops_s - top_s)
        sum_t = jnp.sum(stats[block, :, 2, :] * scale_t, axis=0, keepdims=True)
        cross = jnp.sum(stats[block, :, 3, :] * scale_t, axis=0, keepdims=True)
        sum_s = jnp.sum(stats[block, :, 4, :] * scale_s, axis=0, keepdims=True)
        target = jnp.sum(stats[block, :, 5, :], axis=0, keepdims=True)
        lse_t, lse_s = top_t + jnp.log(sum_t), top_s + jnp.log(sum_s)
        weight = label_row(block, 1).astype(F32)
        loss = weight * (cross / sum_t - lse_t + lse_s + 0.5 * (lse_s - target))
        mine = jnp.zeros((1, PART), F32)
        for slot in range(8):
            mine = jnp.where(me == slot, loss[:, PART * slot : PART * (slot + 1)], mine)
        own_losses.append(mine)
        prob_t = et[block] * (jnp.exp(stats[block, me, 0:1, :] - top_t) / sum_t)
        prob_s = es[block] * (jnp.exp(stats[block, me, 1:2, :] - top_s) / sum_s)
        onehot = (entry == label_row(block, 0)).astype(F32)
        grad = weight * ((prob_s - prob_t) + 0.5 * (prob_s - onehot))
        lg[:, BLOCK * block : BLOCK * (block + 1)] = grad.astype(jnp.bfloat16)
    loss_ref[...] = jnp.concatenate(own_losses, axis=1)

    half_cols = rst.shape[0] // 2
    for j in range(2):
        tile = lax.dot_general(
            rst[half_cols * j : half_cols * (j + 1), :], lg[...], NT, preferred_element_type=F32
        ).reshape(2, NY, 2 * PIECE, SLAB)
        for i in range(4):
            part = jnp.concatenate([tile[a, 2 * i + b, :, :128] for a in (0, 1) for b in (0, 1)], axis=0)
            gpf[4 * j + i] = part
            gpb[4 * j + i] = part.astype(jnp.bfloat16)
        for dz in range(NZ):
            a, b, low = dz // 4, dz // 2 % 2, dz % 2 * PIECE
            part = jnp.concatenate([tile[a, 2 * i + b, low : low + PIECE, 128:] for i in range(4)], axis=0)
            gzf[dz, 4 * PIECE * j : 4 * PIECE * (j + 1)] = part
            gzb[dz, 4 * PIECE * j : 4 * PIECE * (j + 1)] = part.astype(jnp.bfloat16)

    def sum_copies(k):
        to_p, to_z = lax.rem(p + k, 8), lax.rem(z + k, NZ)
        return (
            remote(gpb.at[to_p], yq.at[p], ys_s.at[k], ys_r.at[p], p_dev(to_p)),
            remote(gzb.at[to_z], zq.at[z], zq_s.at[k], zq_r.at[z], dev(x, y, to_z, c)),
        )

    def sum_start(k, _):
        for copy in sum_copies(k):
            copy.start()
        return 0

    lax.fori_loop(1, 8, sum_start, 0)
    ya[...] = gpf[p]
    za[...] = gzf[z]

    def sum_add(k, _):
        from_p, from_z = lax.rem(p + k, 8), lax.rem(z + k, NZ)
        remote(yq.at[from_p], yq.at[from_p], ys_s.at[k], ys_r.at[from_p], sib).wait_recv()
        ya[...] += yq[from_p].astype(F32)
        remote(zq.at[from_z], zq.at[from_z], zq_s.at[k], zq_r.at[from_z], sib).wait_recv()
        za[...] += zq[from_z].astype(F32)
        return 0

    lax.fori_loop(1, 8, sum_add, 0)

    def window(ref, i):
        start = lax.div(i, 2) * 2 * PIECE + lax.rem(i, 2) * 32
        return ref.at[pl.ds(pl.multiple_of(start, 8), WIN)]

    def last_copies(k):
        to_z, to_p = lax.rem(z + k, NZ), lax.rem(p + k, 8)
        return (
            remote(window(ya, to_z), y2.at[z], zr_s.at[k], zr_r.at[z], dev(x, y, to_z, c)),
            remote(window(za, to_p), z2.at[p], yr_s.at[k], yr_r.at[p], p_dev(to_p)),
        )

    def last_start(k, _):
        for copy in last_copies(k):
            copy.start()
        return 0

    def last_wait(k, _):
        from_z, from_p = lax.rem(z + k, NZ), lax.rem(p + k, 8)
        remote(y2.at[from_z], y2.at[from_z], zr_s.at[k], zr_r.at[from_z], sib).wait_recv()
        remote(z2.at[from_p], z2.at[from_p], yr_s.at[k], yr_r.at[from_p], sib).wait_recv()
        return 0

    lax.fori_loop(1, 8, last_start, 0)
    y2[z] = window(ya, z)[...]
    z2[p] = window(za, p)[...]
    lax.fori_loop(1, 8, last_wait, 0)

    def piece_of(ref, odd):
        total = jnp.sum(ref[...], axis=0)
        return jnp.where(odd == 0, total[:PIECE], total[WIN - PIECE :])

    ow[:PIECE] = jnp.concatenate([piece_of(y2, zl), piece_of(z2, lax.rem(p, 2))], axis=1)
    ow[PIECE:] = jnp.zeros((WIN - PIECE, SLAB), F32)

    @pl.when(away)
    def _():
        copy = remote(ow, ox, o_s, o_r, partner)
        copy.start()
        copy.wait()

    @pl.when(jnp.logical_not(away))
    def _():
        ox[...] = ow[...]

    out_ref[...] = ox[:PIECE]

    for a in (0, 1):
        own_to_sib(a).wait_send()
        for q in range(4):
            for m in (1, 2, 3):
                send_rows(q, m, a).wait_send()
                to_sib(q, m, a).wait_send()
    for step in range(4):
        for d in (0, 1):
            for h in (0, 1):
                if step < 3 or h == d:
                    for a in (0, 1):
                        ring_copy(a, d, step, h, False).wait_send()

    def wait_sent(k, _):
        p_copy(k, False).wait_send()
        for q in range(4):
            label_copy(q, k, me).wait_send()
            stats_copy(q, k, me).wait_send()
        for copy in sum_copies(k) + last_copies(k):
            copy.wait_send()
        return 0

    lax.fori_loop(1, 8, wait_sent, 0)


def per_device(teacher_hidden, student_hidden, teacher_head, student_head, targets, row_mask):
    dt, ds = teacher_hidden.shape[1], student_hidden.shape[1]
    rows_t, rows_s = teacher_hidden.reshape(4, PART, dt), student_hidden.reshape(4, PART, ds)
    bf16 = jnp.bfloat16
    dma = pltpu.SemaphoreType.DMA
    anywhere, vmem = pl.BlockSpec(memory_space=pl.ANY), pl.BlockSpec(memory_space=pltpu.VMEM)
    loss, out = pl.pallas_call(
        kernel,
        out_shape=(jax.ShapeDtypeStruct((1, ROWS), F32), jax.ShapeDtypeStruct((PIECE, SLAB), F32)),
        in_specs=[anywhere, anywhere, anywhere, vmem, vmem, vmem],
        out_specs=(vmem, vmem),
        scratch_shapes=[
            pltpu.VMEM((4, 8, PART, dt), bf16),
            pltpu.VMEM((4, 8, PART, ds), bf16),
            pltpu.VMEM((PAD, SLAB), bf16),
            pltpu.VMEM((SLAB, dt), bf16),
            pltpu.VMEM((NZ, NY, PAD, SLAB), bf16),
            pltpu.VMEM((ds, SLAB), bf16),
            pltpu.VMEM((SLAB, ds), bf16),
            pltpu.VMEM((ds, 8 * ROWS), bf16),
            pltpu.VMEM((4, SLAB, BLOCK), F32),
            pltpu.VMEM((4, SLAB, BLOCK), F32),
            pltpu.VMEM((SLAB, 4 * BLOCK), bf16),
            pltpu.VMEM((8, CHUNK, 128), F32),
            pltpu.VMEM((8, CHUNK, 128), bf16),
            pltpu.VMEM((NZ, CHUNK, 128), F32),
            pltpu.VMEM((NZ, CHUNK, 128), bf16),
            pltpu.VMEM((8, CHUNK, 128), bf16),
            pltpu.VMEM((NZ, CHUNK, 128), bf16),
            pltpu.VMEM((CHUNK, 128), F32),
            pltpu.VMEM((CHUNK, 128), F32),
            pltpu.VMEM((NZ, WIN, 128), F32),
            pltpu.VMEM((NY, WIN, 128), F32),
            pltpu.VMEM((WIN, SLAB), F32),
            pltpu.VMEM((WIN, SLAB), F32),
            pltpu.VMEM((4, 8, 8, ROWS), jnp.int32),
            pltpu.VMEM((4, 8, 8, BLOCK), F32),
            dma((4,)),
            dma((4, 8)), dma((4, 8)),
            dma((2,)), dma((2,)),
            dma((8,)), dma((8,)),
            dma((2, 2, 4, 2)), dma((2, 2, 4, 2)),
            dma((4, 3, 2)), dma((4, 3, 2)), dma((4, 3, 2)), dma((4, 3, 2)),
            dma((2,)), dma((2,)),
            dma((4, 8)), dma((4, 8)),
            dma((8,)), dma((8,)), dma((8,)), dma((8,)),
            dma((8,)), dma((8,)), dma((8,)), dma((8,)),
            dma, dma,
        ],
        compiler_params=pltpu.CompilerParams(
            collective_id=0, has_side_effects=True, vmem_limit_bytes=56 * 1024 * 1024
        ),
        cost_estimate=pl.CostEstimate(flops=4_900_000_000, bytes_accessed=6_000_000, transcendentals=1_000_000),
    )(rows_t, rows_s, teacher_head, student_head, targets.reshape(1, ROWS), row_mask.reshape(1, ROWS))
    return loss.reshape(ROWS), out


def solution(mesh):
    in_specs = (
        P(("tok", "voc"), None),
        P(("tok", "voc"), None),
        P("voc", None),
        P("tok", "voc"),
        P(("tok", "voc")),
        P(("tok", "voc")),
    )
    out_specs = (P(("tok", "voc")), P("tok", "voc"))
    return jax.shard_map(
        per_device, mesh=mesh, in_specs=in_specs, out_specs=out_specs, check_vma=False
    )
```

time: 1150 us -> 160 us (0.14); the launches traced: 1130 us -> 159 us
  waiting for transfers between devices: 1030 us -> 0 us
  Pallas kernels: 0 us -> 156 us
  blocking collectives: 61.4 us -> 0 us
  matrix products: 18.5 us -> 0 us
  between operations: 14.5 us -> 0.64 us
    unnamed x5 -> x0, waiting for transfers between devices: 591 us -> none
    all_gather x3 -> x0, waiting for transfers between devices: 439 us -> none  [the longest x1 265 us: per_device(): student_full = lax.all_gather(student_head, 'tok', axis=0, tiled=True)]
    pallas_call x0 -> x1, Pallas kernels: none -> 156 us  [per_device(): pl.pallas_call(kernel, out_shape=(jax.ShapeDtypeStruct((1, ROWS), F32), j...]
    psum x1 -> x0, blocking collectives: 27.2 us -> none  [per_device(): lax.psum((jnp.sum(exp_t, axis=1), jnp.sum(exp_t * (logits_t - logits_s),...]
    dot_general x3 -> x0, matrix products: 18.5 us -> none  [the longest x1 7.28 us: per_device(): jnp.einsum('rd,vd->rv', rows_t, teacher_head, preferred_element_type=jnp....]
    all_gather x1 -> x0, blocking collectives: 17.7 us -> none  [per_device(): lax.all_gather(jnp.stack([targets, row_mask]), 'voc', axis=1, tiled=True)]
    pmax x1 -> x0, blocking collectives: 16.5 us -> none  [per_device(): lax.pmax((jnp.max(logits_t, axis=1), jnp.max(logits_s, axis=1)), 'voc')]
  transfers between devices with their start and end apart: 4 -> 0, of which waited for: 4 -> 0; matrix products, arithmetic and copies ran while one was open for 1% -> 0% of each run, Pallas kernels for 0% -> 0%
where the time goes in v4:
time: 160 us; the launch traced here: 159 us
  Pallas kernels  156 us (98%)
  local copies, waits for them, and re-layouts  2.54 us (2%)
    pallas_call x1, Pallas kernels, per_device(): pl.pallas_call(kernel, out_shape=(jax.ShapeDtypeStruct((1, ROWS), F32), j...  156 us

profile of v4, /device:TPU:6, one launch (start us, length us, event | category | flops | bytes accessed | tf_op | source)
XLA Modules:
  0.0 158.8 jit_solution(2280728829252514829)
XLA Ops:
  0.6 155.6 %shard_map.77 = (f32[1,128]{1,0:T(1,128)}, f32[36,256]{1,0:T(8,128)}) custom-call(bf16[4,32,4608]{2,1,0:T(8,128)(2,1)} %bitcast.5, bf16[4,32,2304]{2,1,0:T(8,128)(2,1)} %bitcast.6, bf16[256,4608]{1,0:T(8,128)(2,1)} %tw.1, bf16[36,256]{1,0:T(8,128)(2,1)} %sw.1, s32[1,128]{1,0:T(1,128)} %bitcast.7, s32[1,128]{1,0:T(1,128)} %bitcast.8), custom_call_target="tpu_custom_call" | custom-call | flops 4899999744 | bytes 6000000 | tf_op jit(solution)/shard_map/pallas_call | solution.py:462
  156.2 1.1 copy.10
  157.4 1.4 copy.11

commit v5 on v3

--- a/solution.py
+++ b/solution.py
@@ -12,7 +12,7 @@
 PIECE = 36
 PAD = 48
 WIN = 40
-TALL, WIN16 = 80, 48
+CHUNK = 8 * PIECE
 MESH = pl.DeviceIdType.MESH
 F32 = jnp.float32
 NT = (((1,), (1,)), ((), ()))
@@ -26,7 +26,7 @@
 
 def kernel(
     th, sh, tw, sw, target_in, mask_in, loss_ref, out_ref,
-    rt, rs, piece_ref, tslab, spad, swt, swr, rst, et, es, lg, g, gb, yq, zq, ya, za, y2, z2, ow, ox, labs, stats, late, losses,
+    rt, rs, piece_ref, tslab, spad, swt, swr, rst, et, es, lg, gyf, gyb, gzf, gzb, yq, zq, ya, za, y2, z2, ow, ox, labs, stats, late, losses,
     loc_sem, lab_s, lab_r, tr_s, tr_r, zt_s, zt_r, zs_s, zs_r, h_s, h_r,
     x_s, x_r, f_s, f_r, b_s, b_r, st_s, st_r, sl_s, sl_r, ys_s, ys_r, zq_s, zq_r, yr_s, yr_r, zr_s, zr_r, o_s, o_r,
 ):
@@ -357,28 +357,26 @@
         lg[:, 2 * ROWS * block : 2 * ROWS * (block + 1)] = grad.astype(jnp.bfloat16)
     loss_ref[...] = losses[me]
 
-    half_cols = g.shape[0] // 2 * g.shape[1] * g.shape[2]
+    half_cols = rst.shape[0] // 2
     for j in range(2):
-        rows_s = rst[half_cols * j : half_cols * (j + 1), :]
-        tile = lax.dot_general(rows_s, lg[...], NT, preferred_element_type=F32)
-        tile = tile.reshape((2,) + g.shape[1:])
-        g[2 * j : 2 * j + 2] = tile
-        rest = jnp.zeros((2, NY, TALL - 2 * PIECE, SLAB), F32)
-        gb[2 * j : 2 * j + 2] = jnp.concatenate([tile, rest], axis=2).astype(jnp.bfloat16)
-
-    def low16(dz):
-        return pl.multiple_of(lax.rem(dz, 2) * 32, 16)
+        tile = lax.dot_general(
+            rst[half_cols * j : half_cols * (j + 1), :], lg[...], NT, preferred_element_type=F32
+        ).reshape(2, NY, 2 * PIECE, SLAB)
+        for i in range(NY):
+            part = jnp.concatenate([tile[0, i, :, :128], tile[1, i, :, :128]], axis=0)
+            gyf[i, 4 * PIECE * j : 4 * PIECE * (j + 1)] = part
+            gyb[i, 4 * PIECE * j : 4 * PIECE * (j + 1)] = part.astype(jnp.bfloat16)
+        for a in (0, 1):
+            for low in (0, 1):
+                part = jnp.concatenate([tile[a, i, low * PIECE : (low + 1) * PIECE, 128:] for i in range(NY)], axis=0)
+                gzf[4 * j + 2 * a + low] = part
+                gzb[4 * j + 2 * a + low] = part.astype(jnp.bfloat16)
 
     def sum_copies(k):
         to_y, to_z = lax.rem(y + k, NY), lax.rem(z + k, NZ)
         return (
-            remote(
-                gb.at[:, to_y, :, pl.ds(0, 128)], yq.at[y], ys_s.at[k], ys_r.at[y], dev(x, to_y, z, c)
-            ),
-            remote(
-                gb.at[lax.div(to_z, 2), :, pl.ds(low16(to_z), WIN16), pl.ds(128, 128)],
-                zq.at[z], zq_s.at[k], zq_r.at[z], dev(x, y, to_z, c),
-            ),
+            remote(gyb.at[to_y], yq.at[y], ys_s.at[k], ys_r.at[y], dev(x, to_y, z, c)),
+            remote(gzb.at[to_z], zq.at[z], zq_s.at[k], zq_r.at[z], dev(x, y, to_z, c)),
         )
 
     def sum_start(k, _):
@@ -387,27 +385,28 @@
         return 0
 
     lax.fori_loop(1, 8, sum_start, 0)
-    ya[...] = g[:, y, :, :128]
-    za[...] = g[zh, :, pl.ds(pl.multiple_of(zl * 32, 8), WIN), 128:]
+    ya[...] = gyf[y]
+    za[...] = gzf[z]
 
     def sum_add(k, _):
         from_y, from_z = lax.rem(y + k, NY), lax.rem(z + k, NZ)
         remote(yq.at[from_y], yq.at[from_y], ys_s.at[k], ys_r.at[from_y], sib).wait_recv()
-        ya[...] += yq[from_y].astype(F32)[:, : 2 * PIECE]
+        ya[...] += yq[from_y].astype(F32)
         remote(zq.at[from_z], zq.at[from_z], zq_s.at[k], zq_r.at[from_z], sib).wait_recv()
-        za[...] += zq[from_z].astype(F32)[:, :WIN]
+        za[...] += zq[from_z].astype(F32)
         return 0
 
     lax.fori_loop(1, 8, sum_add, 0)
 
-    def part_y(dz):
-        return ya.at[lax.div(dz, 2), pl.ds(pl.multiple_of(lax.rem(dz, 2) * 32, 8), WIN)]
+    def window(ref, i):
+        start = lax.div(i, 2) * 2 * PIECE + lax.rem(i, 2) * 32
+        return ref.at[pl.ds(pl.multiple_of(start, 8), WIN)]
 
     def last_copies(k):
         to_z, to_y = lax.rem(z + k, NZ), lax.rem(y + k, NY)
         return (
-            remote(part_y(to_z), y2.at[z], zr_s.at[k], zr_r.at[z], dev(x, y, to_z, c)),
-            remote(za.at[to_y], z2.at[y], yr_s.at[k], yr_r.at[y], dev(x, to_y, z, c)),
+            remote(window(ya, to_z), y2.at[z], zr_s.at[k], zr_r.at[z], dev(x, y, to_z, c)),
+            remote(window(za, to_y), z2.at[y], yr_s.at[k], yr_r.at[y], dev(x, to_y, z, c)),
         )
 
     def last_start(k, _):
@@ -422,10 +421,16 @@
         return 0
 
     lax.fori_loop(1, 8, last_start, 0)
-    y2[z] = part_y(z)[...]
-    z2[y] = za[y]
+    y2[z] = window(ya, z)[...]
+    z2[y] = window(za, y)[...]
     lax.fori_loop(1, 8, last_wait, 0)
-    ow[...] = jnp.concatenate([jnp.sum(y2[...], axis=0), jnp.sum(z2[...], axis=0)], axis=1)
+
+    def piece_of(ref, odd):
+        total = jnp.sum(ref[...], axis=0)
+        return jnp.where(odd == 0, total[:PIECE], total[WIN - PIECE :])
+
+    ow[:PIECE] = jnp.concatenate([piece_of(y2, zl), piece_of(z2, lax.rem(y, 2))], axis=1)
+    ow[PIECE:] = jnp.zeros((WIN - PIECE, SLAB), F32)
 
     @pl.when(away)
     def _():
@@ -437,7 +442,7 @@
     def _():
         ox[...] = ow[...]
 
-    out_ref[...] = jnp.where(zl == 0, ox[:PIECE], ox[WIN - PIECE :])
+    out_ref[...] = ox[:PIECE]
 
     for d in (0, 1):
         for a in (0, 1):
@@ -490,12 +495,14 @@
             pltpu.VMEM((NX, SLAB, 2 * ROWS), F32),
             pltpu.VMEM((NX, SLAB, 2 * ROWS), F32),
             pltpu.VMEM((SLAB, 8 * ROWS), bf16),
-            pltpu.VMEM((NX, NY, 2 * PIECE, SLAB), F32),
-            pltpu.VMEM((NX, NY, TALL, SLAB), bf16),
-            pltpu.VMEM((NY, NX, TALL, 128), bf16),
-            pltpu.VMEM((NZ, NY, WIN16, 128), bf16),
-            pltpu.VMEM((NX, 2 * PIECE, 128), F32),
-            pltpu.VMEM((NY, WIN, 128), F32),
+            pltpu.VMEM((NY, CHUNK, 128), F32),
+            pltpu.VMEM((NY, CHUNK, 128), bf16),
+            pltpu.VMEM((NZ, CHUNK, 128), F32),
+            pltpu.VMEM((NZ, CHUNK, 128), bf16),
+            pltpu.VMEM((NY, CHUNK, 128), bf16),
+            pltpu.VMEM((NZ, CHUNK, 128), bf16),
+            pltpu.VMEM((CHUNK, 128), F32),
+            pltpu.VMEM((CHUNK, 128), F32),
             pltpu.VMEM((NZ, WIN, 128), F32),
             pltpu.VMEM((NY, WIN, 128), F32),
             pltpu.VMEM((WIN, SLAB), F32),

time: 125 us -> 121 us (0.968)
  Pallas kernels: 121 us -> 117 us
    pallas_call x1, Pallas kernels: 121 us -> 117 us  [per_device(): pl.pallas_call(kernel, out_shape=(jax.ShapeDtypeStruct((1, ROWS), F32), j...]
where the time goes in v5:
time: 121 us; the launch traced here: 120 us
  Pallas kernels  117 us (97%)
  local copies, waits for them, and re-layouts  2.54 us (2%)
    pallas_call x1, Pallas kernels, per_device(): pl.pallas_call(kernel, out_shape=(jax.ShapeDtypeStruct((1, ROWS), F32), j...  117 us
    unnamed x2, local copies, waits for them, and re-layouts  2.54 us

profile of v5, /device:TPU:6, one launch (start us, length us, event | category | flops | bytes accessed | tf_op | source)
XLA Modules:
  0.0 120.3 jit_solution(7233335336363773442)
XLA Ops:
  0.6 117.2 %shard_map.77 = (f32[1,128]{1,0:T(1,128)}, f32[36,256]{1,0:T(8,128)}) custom-call(bf16[128,4608]{1,0:T(8,128)(2,1)} %th.1, bf16[128,2304]{1,0:T(8,128)(2,1)} %sh.1, bf16[256,4608]{1,0:T(8,128)(2,1)} %tw.1, bf16[36,256]{1,0:T(8,128)(2,1)} %sw.1, s32[1,128]{1,0:T(1,128)} %bitcast.3, s32[1,128]{1,0:T(1,128)} %bitcast.4), custom_call_target="tpu_custom_call" | custom-call | flops 4899999744 | bytes 6000000 | tf_op jit(solution)/shard_map/pallas_call | solution.py:481
  117.8 1.1 copy.10
  118.9 1.4 %copy.11 = f32[36,256]{1,0:T(8,128)} copy(f32[36,256]{1,0:T(8,128)} %get-tuple-element.9) | data formatting | bytes 73728

commit v6 on v5

--- a/solution.py
+++ b/solution.py
@@ -13,6 +13,7 @@
 PAD = 48
 WIN = 40
 CHUNK = 8 * PIECE
+FAR_FIRST = (4, 3, 5, 2, 6, 1, 7)
 MESH = pl.DeviceIdType.MESH
 F32 = jnp.float32
 NT = (((1,), (1,)), ((), ()))
@@ -25,7 +26,7 @@
 
 
 def kernel(
-    th, sh, tw, sw, target_in, mask_in, loss_ref, out_ref,
+    th, sh, tw, sw, target_in, mask_in, out_ref,
     rt, rs, piece_ref, tslab, spad, swt, swr, rst, et, es, lg, gyf, gyb, gzf, gzb, yq, zq, ya, za, y2, z2, ow, ox, labs, stats, late, losses,
     loc_sem, lab_s, lab_r, tr_s, tr_r, zt_s, zt_r, zs_s, zs_r, h_s, h_r,
     x_s, x_r, f_s, f_r, b_s, b_r, st_s, st_r, sl_s, sl_r, ys_s, ys_r, zq_s, zq_r, yr_s, yr_r, zr_s, zr_r, o_s, o_r,
@@ -102,16 +103,6 @@
             pltpu.make_async_copy(piece_ref, dst_s, loc_sem.at[3]),
         )
 
-    @pl.when(away)
-    def _():
-        for copy in turn_copies():
-            copy.start()
-
-    @pl.when(jnp.logical_not(away))
-    def _():
-        for copy in turn_local():
-            copy.start()
-
     def half(ref, block, h):
         return ref.at[block, pl.ds(h * HALF, HALF)]
 
@@ -150,9 +141,19 @@
         return remote(src.at[pl.ds(h * HALF, HALF)], half(dst, me, h), b_s.at[0, h, a], b_r.at[0, h, a], sib)
 
     for first in (0, 1):
-        for a in (0, 1):
+        for a in (1, 0):
             send_own(0, first, a).start()
             send_own(1, 1 - first, a).start()
+    @pl.when(away)
+    def _():
+        for copy in turn_copies():
+            copy.start()
+
+    @pl.when(jnp.logical_not(away))
+    def _():
+        for copy in turn_local():
+            copy.start()
+
     for h in (0, 1):
         for a in (0, 1):
             own_to_sib(h, a).start()
@@ -225,7 +226,7 @@
 
     ring_step(0)
     ring_step(1)
-    for a in (0, 1):
+    for a in (1, 0):
         for d in (0, 1):
             came_own(d, d, a).wait_recv()
             pass_on(d, a).start()
@@ -322,7 +323,7 @@
         return 0
 
     lax.fori_loop(1, 8, send_early, 0)
-    for a in (0, 1):
+    for a in (1, 0):
         for d in (0, 1):
             came_on(d, a).wait_recv()
             to_sib(3, xo, d, a).start()
@@ -355,7 +356,7 @@
         onehot = (entry == label_row(block, 0)).astype(F32)
         grad = weight * ((prob_s - prob_t) + 0.5 * (prob_s - onehot))
         lg[:, 2 * ROWS * block : 2 * ROWS * (block + 1)] = grad.astype(jnp.bfloat16)
-    loss_ref[...] = losses[me]
+    own_loss = losses[me]
 
     half_cols = rst.shape[0] // 2
     for j in range(2):
@@ -384,7 +385,8 @@
             copy.start()
         return 0
 
-    lax.fori_loop(1, 8, sum_start, 0)
+    for k in FAR_FIRST:
+        sum_start(k, 0)
     ya[...] = gyf[y]
     za[...] = gzf[z]
 
@@ -420,7 +422,8 @@
         remote(z2.at[from_y], z2.at[from_y], yr_s.at[k], yr_r.at[from_y], sib).wait_recv()
         return 0
 
-    lax.fori_loop(1, 8, last_start, 0)
+    for k in FAR_FIRST:
+        last_start(k, 0)
     y2[z] = window(ya, z)[...]
     z2[y] = window(za, y)[...]
     lax.fori_loop(1, 8, last_wait, 0)
@@ -431,6 +434,7 @@
 
     ow[:PIECE] = jnp.concatenate([piece_of(y2, zl), piece_of(z2, lax.rem(y, 2))], axis=1)
     ow[PIECE:] = jnp.zeros((WIN - PIECE, SLAB), F32)
+    out_ref[PIECE:] = jnp.zeros((WIN - PIECE, SLAB), F32)
 
     @pl.when(away)
     def _():
@@ -442,7 +446,8 @@
     def _():
         ox[...] = ow[...]
 
-    out_ref[...] = ox[:PIECE]
+    out_ref[:PIECE] = ox[:PIECE]
+    out_ref[PIECE : PIECE + 1] = jnp.concatenate([own_loss, own_loss], axis=1)
 
     for d in (0, 1):
         for a in (0, 1):
@@ -478,11 +483,11 @@
     bf16 = jnp.bfloat16
     dma = pltpu.SemaphoreType.DMA
     anywhere, vmem = pl.BlockSpec(memory_space=pl.ANY), pl.BlockSpec(memory_space=pltpu.VMEM)
-    loss, out = pl.pallas_call(
+    out = pl.pallas_call(
         kernel,
-        out_shape=(jax.ShapeDtypeStruct((1, ROWS), F32), jax.ShapeDtypeStruct((PIECE, SLAB), F32)),
+        out_shape=jax.ShapeDtypeStruct((WIN, SLAB), F32),
         in_specs=[anywhere, anywhere, anywhere, vmem, vmem, vmem],
-        out_specs=(vmem, vmem),
+        out_specs=vmem,
         scratch_shapes=[
             pltpu.VMEM((8, ROWS, dt), bf16),
             pltpu.VMEM((8, ROWS, ds), bf16),
@@ -529,7 +534,7 @@
         ),
         cost_estimate=pl.CostEstimate(flops=4_900_000_000, bytes_accessed=6_000_000, transcendentals=1_000_000),
     )(teacher_hidden, student_hidden, teacher_head, student_head, targets.reshape(1, ROWS), row_mask.reshape(1, ROWS))
-    return loss.reshape(ROWS), out
+    return out[PIECE, :ROWS], out[:PIECE]
 
 
 def solution(mesh):

time: 121 us -> 117 us (0.967)
  Pallas kernels: 117 us -> 113 us
    pallas_call x1, Pallas kernels: 117 us -> 113 us  [per_device(): pl.pallas_call(kernel, out_shape=jax.ShapeDtypeStruct((WIN, SLAB), F32),...]
    unnamed x2 -> x1, local copies, waits for them, and re-layouts: 2.54 us -> 1.4 us
where the time goes in v6:
time: 117 us; the launch traced here: 116 us
  Pallas kernels  113 us (97%)
  local copies, waits for them, and re-layouts  2.58 us (2%)
    pallas_call x1, Pallas kernels, per_device(): pl.pallas_call(kernel, out_shape=jax.ShapeDtypeStruct((WIN, SLAB), F32),...  113 us

profile of v6, /device:TPU:6, one launch (start us, length us, event | category | flops | bytes accessed | tf_op | source)
XLA Modules:
  0.0 116.4 jit_solution(2358792785019510037)
XLA Ops:
  0.6 113.2 %shard_map.77 = f32[40,256]{1,0:T(8,128)} custom-call(bf16[128,4608]{1,0:T(8,128)(2,1)} %th.1, bf16[128,2304]{1,0:T(8,128)(2,1)} %sh.1, bf16[256,4608]{1,0:T(8,128)(2,1)} %tw.1, bf16[36,256]{1,0:T(8,128)(2,1)} %sw.1, s32[1,128]{1,0:T(1,128)} %bitcast.6, s32[1,128]{1,0:T(1,128)} %bitcast.7), custom_call_target="tpu_custom_call" | custom-call | flops 4899999744 | bytes 6000000 | tf_op jit(solution)/shard_map/pallas_call | solution.py:486
  113.8 1.2 %slice_bitcast_fusion = f32[128]{0:T(128)} fusion(f32[40,256]{1,0:T(8,128)} %shard_map.77), kind=kLoop, calls=%fused_computation | loop fusion | bytes 1024 | tf_op jit(solution)/shard_map/squeeze | solution.py:537
  115.0 1.4 %copy.9 = f32[36,256]{1,0:T(8,128)} copy(f32[36,256]{1,0:T(8,128)} %bitcast.5) | data formatting | bytes 73728
